TPU v7x, 512 devices: a whole 4x8x8 slice. The times are simulated.
512 devices in a mesh: chan: 64 (over x, y, z_lo), sp: 8 (over z_hi, core).
Axes of the slice: x: 4, y: 8, z: 8 (z_hi: 4, z_lo: 2; z = z_hi * 2 + z_lo), core: 2. Of those that a mesh axis runs over, the one named last changes fastest.
Arguments:
- activations: bfloat16 [16, 64, 64, 256], P('sp', 'chan'), may hold values from -16 to 16
- weights: bfloat16 [27, 256, 256], replicated, may hold values from -0.078125 to 0.078125
- grad_output: bfloat16 [16, 64, 64, 256], P('sp', 'chan'), may hold values from -6 to 6
Outputs:
- output: bfloat16 [16, 64, 64, 256], P('sp', 'chan')
- grad_input: bfloat16 [16, 64, 64, 256], P('sp', 'chan')
- grad_weights: float32 [27, 256, 256], P(None, 'chan')
All inputs are finite; a program needn't handle non-finite values.
Results may differ from a plain program's by a relative error of at most 0.001.
Values may be sent and summed in bfloat16 or wider, within the bound.
A program may use at most 64 MiB of HBM per device.

v0:
```python
import jax
import jax.numpy as jnp
from jax import lax
from jax.sharding import PartitionSpec as P


def padded(block, sides, width):
    for axis, dim in sides:
        count = lax.axis_size(axis)
        forward = [(i, i + 1) for i in range(count - 1)]
        backward = [(target, source) for source, target in forward]
        low = lax.ppermute(
            lax.slice_in_dim(block, block.shape[dim] - width, None, axis=dim), axis, forward
        )
        high = lax.ppermute(lax.slice_in_dim(block, 0, width, axis=dim), axis, backward)
        block = jnp.concatenate([low, block, high], axis=dim)
    return block


def passed_along(value, axis, steps):
    count = lax.axis_size(axis)
    pairs = [(source, (source + steps) % count) for source in range(count)]
    return lax.ppermute(value, axis, pairs)


def tap_offsets(tap_index):
    return (tap_index // 9, tap_index // 3 % 3, tap_index % 3)


def on_device(activations, weights, grad_output):
    plane_count, row_count, column_count, channels = activations.shape
    out_channels = grad_output.shape[3]
    cell_count = plane_count * row_count * column_count
    near_act, near_grad = (
        padded(activations, (("chan", 1), ("sp", 0)), 1),
        padded(grad_output, (("chan", 1), ("sp", 0)), 1),
    )
    side_pad = ((0, 0), (0, 0), (1, 1), (0, 0))
    pad_act = jnp.pad(near_act, side_pad)
    pad_grad = jnp.pad(near_grad, side_pad)
    flat_grad = grad_output.reshape(cell_count, out_channels)

    def act_window(source, tap_index):
        plane_off, row_off, col_off = tap_offsets(tap_index)
        part = source[
            plane_off : plane_off + plane_count,
            row_off : row_off + row_count,
            col_off : col_off + column_count,
        ]
        return part.reshape(cell_count, source.shape[3])

    produced = jnp.zeros((cell_count, out_channels), jnp.float32)
    gradient_rows = jnp.zeros((cell_count, channels), jnp.float32)
    for tap_index in range(27):
        plane_off, row_off, col_off = tap_offsets(tap_index)
        produced = produced + jnp.dot(
            act_window(pad_act, tap_index), weights[tap_index], preferred_element_type=jnp.float32
        )
        grad_window = pad_grad[
            2 - plane_off : 2 - plane_off + plane_count,
            2 - row_off : 2 - row_off + row_count,
            2 - col_off : 2 - col_off + column_count,
        ].reshape(cell_count, out_channels)
        gradient_rows = gradient_rows + lax.dot_general(
            grad_window,
            weights[tap_index],
            (((1,), (1,)), ((), ())),
            preferred_element_type=jnp.float32,
        )
    cycle_size = lax.axis_size("chan")
    cycle_index = lax.axis_index("chan")
    slab_width = channels // cycle_size
    patches = jnp.stack([act_window(pad_act, tap_index) for tap_index in range(27)], axis=1)

    def slab_term(slab_number, col_start, col_stop):
        part_patch = lax.dynamic_slice_in_dim(patches, slab_number * slab_width, slab_width, 2)
        flat_patch = part_patch.reshape(cell_count, 27 * slab_width)
        product = lax.dot_general(
            flat_patch, flat_grad, (((0,), (0,)), ((), ())), preferred_element_type=jnp.float32
        )
        return product.reshape(27, slab_width, col_stop - col_start)

    accumulated = slab_term((cycle_index - 1) % cycle_size, 0, out_channels)

    def cycle_step(step_number, carried):
        arrived = passed_along(carried, "chan", 1)
        return arrived + slab_term((cycle_index - step_number - 1) % cycle_size, 0, out_channels)

    accumulated = lax.fori_loop(1, cycle_size, cycle_step, accumulated)
    summed = lax.psum(accumulated, "sp")
    voxel_count = cell_count * cycle_size * lax.axis_size("sp")
    grad_weights = summed * float(voxel_count) ** (-0.5)
    output = produced.reshape(plane_count, row_count, column_count, out_channels).astype(
        jnp.bfloat16
    )
    grad_input = gradient_rows.reshape(plane_count, row_count, column_count, channels).astype(
        jnp.bfloat16
    )
    return (output, grad_input, grad_weights)


def solution(mesh):
    return jax.shard_map(
        on_device,
        mesh=mesh,
        in_specs=(P("sp", "chan", None, None), P(), P("sp", "chan", None, None)),
        out_specs=(P("sp", "chan", None, None), P("sp", "chan", None, None), P(None, "chan", None)),
        check_vma=False,
    )
```

profile of v0, /device:TPU:1, one launch (start us, length us, event | category | flops | bytes accessed | tf_op | source)
XLA Modules:
  0.0 1017.4 jit_solution(3232019523758154982)
XLA Ops:
  8.8 6.1 collective-permute-start.1
  14.9 4.3 collective-permute-start.5
  21.4 5.5 collective-permute-start.4
  35.1 4.5 collective-permute-start.7
  98.0 770.0 %while.15 = (s32[]{:T(128)}, f32[27,4,256]{2,0,1:T(8,128)}, s32[]{:T(128)}, bf16[128,27,256]{0,2,1:T(8,128)(2,1)}, bf16[128,256]{1,0:T(8,128)(2,1)}, /*index=5*/...) while((s32[]{:T(128)}, f32[27,4,256]{2,0,1:T(8,128)}, ...), condition=%wide.region_1.2_spmd, body=%wide.region_0.1_spmd.sunk | while | flops 7105555 | bytes 922964 | solution.py:89
  98.0 4.3 collective-permute-start
  116.2 5.0 collective-permute-done
  129.0 5.1 collective-permute-done
  142.1 4.1 collective-permute-done
  154.1 4.1 collective-permute-done
  166.0 4.1 collective-permute-done
  250.0 4.3 collective-permute-done
  262.1 5.6 collective-permute-done
  275.6 5.0 collective-permute-done
  288.4 4.1 collective-permute-done
  396.4 4.4 collective-permute-done
  408.7 5.7 collective-permute-done
  422.3 4.9 collective-permute-done
  483.0 4.1 collective-permute-done
  495.0 4.1 collective-permute-done
  507.0 4.1 collective-permute-done
  519.0 4.1 collective-permute-done
  543.0 4.5 collective-permute-done
  555.4 5.6 collective-permute-done
  568.9 4.8 collective-permute-done
  689.5 4.6 collective-permute-done
  702.0 5.5 collective-permute-done
  715.4 4.6 collective-permute-done
  835.8 4.8 collective-permute-done
  848.5 5.4 collective-permute-done
  861.8 4.5 collective-permute-done
  885.7 123.3 %all-reduce.4.cloned.1.call-done = f32[27,4,256]{2,1,0:T(4,128)} async-done(((f32[27,4,256]{2,1,0:T(4,128)}), f32[27,4,256]{2,1,0:T(4,128)}) %all-reduce.4.cloned.1.call-update) | async-done | bytes 110608 | tf_op jit(solution)/shard_map/psum | solution.py:90
  (576 shorter events, 734.7 us)
Async XLA Ops:
  7.2 1001.8 %all-reduce.4.cloned.1.call-start = ((), (), s32[]{:S(2)}) async-start(), calls=%async_computation | async-start | bytes 221184 | tf_op jit(solution)/shard_map/psum | solution.py:90
  7.2 13.2 %collective-permute-start.2 = (bf16[2,1,64,256]{3,2,0,1:T(8,128)(2,1)}, bf16[2,1,64,256]{3,2,0,1:T(8,128)(2,1)}, u32[]{:S(2)}, u32[]{:S(2)}) collective-permute-start(bf16[2,1,64,256]{3,2,0,1:T(8,128)(2,1)} %bitcast.299), channel_id=1, source_target_pairs={{8,0},{16,8},{24,16},{32,24},{40,32},{48,40},{56,48},{64,56},{72,6... | collective-permute-start | bytes 196616 | tf_op jit(solution)/shard_map/ppermute | solution.py:15
  8.8 11.7 %collective-permute-start.1 = (bf16[2,1,64,256]{3,2,0,1:T(8,128)(2,1)}, bf16[2,1,64,256]{3,2,0,1:T(8,128)(2,1)}, u32[]{:S(2)}, u32[]{:S(2)}) collective-permute-start(bf16[2,1,64,256]{3,2,0,1:T(8,128)(2,1)} %bitcast.300), channel_id=1, source_target_pairs={{0,8},{8,16},{16,24},{24,32},{32,40},{40,48},{48,56},{56,64},{64,7... | collective-permute-start | bytes 196616 | tf_op jit(solution)/shard_map/ppermute | solution.py:12
  14.9 15.7 %collective-permute-start.5 = (bf16[2,1,64,256]{3,2,1,0:T(8,128)(2,1)}, bf16[2,1,64,256]{3,2,1,0:T(8,128)(2,1)}, u32[]{:S(2)}, u32[]{:S(2)}) collective-permute-start(bf16[2,1,64,256]{3,2,1,0:T(8,128)(2,1)} %param.7), channel_id=1, source_target_pairs={{0,8},{8,16},{16,24},{24,32},{32,40},{40,48},{48,56},{56,64},{64,7... | collective-permute-start | bytes 196616 | tf_op jit(solution)/shard_map/ppermute | solution.py:12
  19.1 13.1 %collective-permute-start.6 = (bf16[2,1,64,256]{3,2,1,0:T(8,128)(2,1)}, bf16[2,1,64,256]{3,2,1,0:T(8,128)(2,1)}, u32[]{:S(2)}, u32[]{:S(2)}) collective-permute-start(bf16[2,1,64,256]{3,2,1,0:T(8,128)(2,1)} %param.7), channel_id=1, source_target_pairs={{8,0},{16,8},{24,16},{32,24},{40,32},{48,40},{56,48},{64,56},{72,6... | collective-permute-start | bytes 196616 | tf_op jit(solution)/shard_map/ppermute | solution.py:15
  21.4 18.2 %collective-permute-start.4 = (bf16[1,3,64,256]{3,2,0,1:T(8,128)(2,1)S(1)}, bf16[1,3,64,256]{3,2,0,1:T(8,128)(2,1)S(1)}, u32[]{:S(2)}, u32[]{:S(2)}) collective-permute-start(bf16[1,3,64,256]{3,2,0,1:T(8,128)(2,1)S(1)} %get-tuple-element.213), channel_id=1, source_target_pairs={{1,0},{2,1},{3,2},{4,3},{5,4},{6,5},{7,6},{9,8},{10,9},{11,10},{12... | collective-permute-start | bytes 294920 | tf_op jit(solution)/shard_map/ppermute | solution.py:15
  27.0 12.7 %collective-permute-start.3 = (bf16[1,3,64,256]{3,2,0,1:T(8,128)(2,1)S(1)}, bf16[1,3,64,256]{3,2,0,1:T(8,128)(2,1)S(1)}, u32[]{:S(2)}, u32[]{:S(2)}) collective-permute-start(bf16[1,3,64,256]{3,2,0,1:T(8,128)(2,1)S(1)} %get-tuple-element.212), channel_id=1, source_target_pairs={{0,1},{1,2},{2,3},{3,4},{4,5},{5,6},{6,7},{8,9},{9,10},{10,11},{11... | collective-permute-start | bytes 294920 | tf_op jit(solution)/shard_map/ppermute | solution.py:12
  33.1 14.4 %collective-permute-start.8 = (bf16[1,3,64,256]{3,2,1,0:T(8,128)(2,1)S(1)}, bf16[1,3,64,256]{3,2,1,0:T(8,128)(2,1)S(1)}, u32[]{:S(2)}, u32[]{:S(2)}) collective-permute-start(bf16[1,3,64,256]{3,2,1,0:T(8,128)(2,1)S(1)} %get-tuple-element.211), channel_id=1, source_target_pairs={{1,0},{2,1},{3,2},{4,3},{5,4},{6,5},{7,6},{9,8},{10,9},{11,10},{12... | collective-permute-start | bytes 294920 | tf_op jit(solution)/shard_map/ppermute | solution.py:15
  35.1 12.5 %collective-permute-start.7 = (bf16[1,3,64,256]{3,2,1,0:T(8,128)(2,1)S(1)}, bf16[1,3,64,256]{3,2,1,0:T(8,128)(2,1)S(1)}, u32[]{:S(2)}, u32[]{:S(2)}) collective-permute-start(bf16[1,3,64,256]{3,2,1,0:T(8,128)(2,1)S(1)} %get-tuple-element.210), channel_id=1, source_target_pairs={{0,1},{1,2},{2,3},{3,4},{4,5},{5,6},{6,7},{8,9},{9,10},{10,11},{11... | collective-permute-start | bytes 294920 | tf_op jit(solution)/shard_map/ppermute | solution.py:12
  98.0 10.2 %collective-permute-start = (f32[27,4,256]{2,0,1:T(8,128)}, f32[27,4,256]{2,0,1:T(8,128)}, u32[]{:S(2)}, u32[]{:S(2)}) collective-permute-start(f32[27,4,256]{2,0,1:T(8,128)} %get-tuple-element.258), channel_id=1, source_target_pairs={{0,8},{8,16},{16,24},{24,32},{32,40},{40,48},{48,56},{56,64},{64,7... | collective-permute-start | bytes 331784 | tf_op jit(solution)/shard_map/while/body/eval_jaxpr/ppermute | solution.py:23
  110.0 11.1 %collective-permute-start = (f32[27,4,256]{2,0,1:T(8,128)}, f32[27,4,256]{2,0,1:T(8,128)}, u32[]{:S(2)}, u32[]{:S(2)}) collective-permute-start(f32[27,4,256]{2,0,1:T(8,128)} %get-tuple-element.258), channel_id=1, source_target_pairs={{0,8},{8,16},{16,24},{24,32},{32,40},{40,48},{48,56},{56,64},{64,7... | collective-permute-start | bytes 331784 | tf_op jit(solution)/shard_map/while/body/eval_jaxpr/ppermute | solution.py:23
  122.9 11.3 %collective-permute-start = (f32[27,4,256]{2,0,1:T(8,128)}, f32[27,4,256]{2,0,1:T(8,128)}, u32[]{:S(2)}, u32[]{:S(2)}) collective-permute-start(f32[27,4,256]{2,0,1:T(8,128)} %get-tuple-element.258), channel_id=1, source_target_pairs={{0,8},{8,16},{16,24},{24,32},{32,40},{40,48},{48,56},{56,64},{64,7... | collective-permute-start | bytes 331784 | tf_op jit(solution)/shard_map/while/body/eval_jaxpr/ppermute | solution.py:23
  135.9 10.2 %collective-permute-start = (f32[27,4,256]{2,0,1:T(8,128)}, f32[27,4,256]{2,0,1:T(8,128)}, u32[]{:S(2)}, u32[]{:S(2)}) collective-permute-start(f32[27,4,256]{2,0,1:T(8,128)} %get-tuple-element.258), channel_id=1, source_target_pairs={{0,8},{8,16},{16,24},{24,32},{32,40},{40,48},{48,56},{56,64},{64,7... | collective-permute-start | bytes 331784 | tf_op jit(solution)/shard_map/while/body/eval_jaxpr/ppermute | solution.py:23
  147.9 10.2 %collective-permute-start = (f32[27,4,256]{2,0,1:T(8,128)}, f32[27,4,256]{2,0,1:T(8,128)}, u32[]{:S(2)}, u32[]{:S(2)}) collective-permute-start(f32[27,4,256]{2,0,1:T(8,128)} %get-tuple-element.258), channel_id=1, source_target_pairs={{0,8},{8,16},{16,24},{24,32},{32,40},{40,48},{48,56},{56,64},{64,7... | collective-permute-start | bytes 331784 | tf_op jit(solution)/shard_map/while/body/eval_jaxpr/ppermute | solution.py:23
  159.9 10.2 %collective-permute-start = (f32[27,4,256]{2,0,1:T(8,128)}, f32[27,4,256]{2,0,1:T(8,128)}, u32[]{:S(2)}, u32[]{:S(2)}) collective-permute-start(f32[27,4,256]{2,0,1:T(8,128)} %get-tuple-element.258), channel_id=1, source_target_pairs={{0,8},{8,16},{16,24},{24,32},{32,40},{40,48},{48,56},{56,64},{64,7... | collective-permute-start | bytes 331784 | tf_op jit(solution)/shard_map/while/body/eval_jaxpr/ppermute | solution.py:23
  243.9 10.4 %collective-permute-start = (f32[27,4,256]{2,0,1:T(8,128)}, f32[27,4,256]{2,0,1:T(8,128)}, u32[]{:S(2)}, u32[]{:S(2)}) collective-permute-start(f32[27,4,256]{2,0,1:T(8,128)} %get-tuple-element.258), channel_id=1, source_target_pairs={{0,8},{8,16},{16,24},{24,32},{32,40},{40,48},{48,56},{56,64},{64,7... | collective-permute-start | bytes 331784 | tf_op jit(solution)/shard_map/while/body/eval_jaxpr/ppermute | solution.py:23
  256.0 11.7 %collective-permute-start = (f32[27,4,256]{2,0,1:T(8,128)}, f32[27,4,256]{2,0,1:T(8,128)}, u32[]{:S(2)}, u32[]{:S(2)}) collective-permute-start(f32[27,4,256]{2,0,1:T(8,128)} %get-tuple-element.258), channel_id=1, source_target_pairs={{0,8},{8,16},{16,24},{24,32},{32,40},{40,48},{48,56},{56,64},{64,7... | collective-permute-start | bytes 331784 | tf_op jit(solution)/shard_map/while/body/eval_jaxpr/ppermute | solution.py:23
  269.5 11.1 %collective-permute-start = (f32[27,4,256]{2,0,1:T(8,128)}, f32[27,4,256]{2,0,1:T(8,128)}, u32[]{:S(2)}, u32[]{:S(2)}) collective-permute-start(f32[27,4,256]{2,0,1:T(8,128)} %get-tuple-element.258), channel_id=1, source_target_pairs={{0,8},{8,16},{16,24},{24,32},{32,40},{40,48},{48,56},{56,64},{64,7... | collective-permute-start | bytes 331784 | tf_op jit(solution)/shard_map/while/body/eval_jaxpr/ppermute | solution.py:23
  282.3 10.2 %collective-permute-start = (f32[27,4,256]{2,0,1:T(8,128)}, f32[27,4,256]{2,0,1:T(8,128)}, u32[]{:S(2)}, u32[]{:S(2)}) collective-permute-start(f32[27,4,256]{2,0,1:T(8,128)} %get-tuple-element.258), channel_id=1, source_target_pairs={{0,8},{8,16},{16,24},{24,32},{32,40},{40,48},{48,56},{56,64},{64,7... | collective-permute-start | bytes 331784 | tf_op jit(solution)/shard_map/while/body/eval_jaxpr/ppermute | solution.py:23
  390.2 10.6 %collective-permute-start = (f32[27,4,256]{2,0,1:T(8,128)}, f32[27,4,256]{2,0,1:T(8,128)}, u32[]{:S(2)}, u32[]{:S(2)}) collective-permute-start(f32[27,4,256]{2,0,1:T(8,128)} %get-tuple-element.258), channel_id=1, source_target_pairs={{0,8},{8,16},{16,24},{24,32},{32,40},{40,48},{48,56},{56,64},{64,7... | collective-permute-start | bytes 331784 | tf_op jit(solution)/shard_map/while/body/eval_jaxpr/ppermute | solution.py:23
  402.6 11.9 %collective-permute-start = (f32[27,4,256]{2,0,1:T(8,128)}, f32[27,4,256]{2,0,1:T(8,128)}, u32[]{:S(2)}, u32[]{:S(2)}) collective-permute-start(f32[27,4,256]{2,0,1:T(8,128)} %get-tuple-element.258), channel_id=1, source_target_pairs={{0,8},{8,16},{16,24},{24,32},{32,40},{40,48},{48,56},{56,64},{64,7... | collective-permute-start | bytes 331784 | tf_op jit(solution)/shard_map/while/body/eval_jaxpr/ppermute | solution.py:23
  416.2 11.0 %collective-permute-start = (f32[27,4,256]{2,0,1:T(8,128)}, f32[27,4,256]{2,0,1:T(8,128)}, u32[]{:S(2)}, u32[]{:S(2)}) collective-permute-start(f32[27,4,256]{2,0,1:T(8,128)} %get-tuple-element.258), channel_id=1, source_target_pairs={{0,8},{8,16},{16,24},{24,32},{32,40},{40,48},{48,56},{56,64},{64,7... | collective-permute-start | bytes 331784 | tf_op jit(solution)/shard_map/while/body/eval_jaxpr/ppermute | solution.py:23
  429.0 10.2 %collective-permute-start = (f32[27,4,256]{2,0,1:T(8,128)}, f32[27,4,256]{2,0,1:T(8,128)}, u32[]{:S(2)}, u32[]{:S(2)}) collective-permute-start(f32[27,4,256]{2,0,1:T(8,128)} %get-tuple-element.258), channel_id=1, source_target_pairs={{0,8},{8,16},{16,24},{24,32},{32,40},{40,48},{48,56},{56,64},{64,7... | collective-permute-start | bytes 331784 | tf_op jit(solution)/shard_map/while/body/eval_jaxpr/ppermute | solution.py:23
  536.9 10.7 %collective-permute-start = (f32[27,4,256]{2,0,1:T(8,128)}, f32[27,4,256]{2,0,1:T(8,128)}, u32[]{:S(2)}, u32[]{:S(2)}) collective-permute-start(f32[27,4,256]{2,0,1:T(8,128)} %get-tuple-element.258), channel_id=1, source_target_pairs={{0,8},{8,16},{16,24},{24,32},{32,40},{40,48},{48,56},{56,64},{64,7... | collective-permute-start | bytes 331784 | tf_op jit(solution)/shard_map/while/body/eval_jaxpr/ppermute | solution.py:23
  549.3 11.8 %collective-permute-start = (f32[27,4,256]{2,0,1:T(8,128)}, f32[27,4,256]{2,0,1:T(8,128)}, u32[]{:S(2)}, u32[]{:S(2)}) collective-permute-start(f32[27,4,256]{2,0,1:T(8,128)} %get-tuple-element.258), channel_id=1, source_target_pairs={{0,8},{8,16},{16,24},{24,32},{32,40},{40,48},{48,56},{56,64},{64,7... | collective-permute-start | bytes 331784 | tf_op jit(solution)/shard_map/while/body/eval_jaxpr/ppermute | solution.py:23
  562.8 10.9 %collective-permute-start = (f32[27,4,256]{2,0,1:T(8,128)}, f32[27,4,256]{2,0,1:T(8,128)}, u32[]{:S(2)}, u32[]{:S(2)}) collective-permute-start(f32[27,4,256]{2,0,1:T(8,128)} %get-tuple-element.258), channel_id=1, source_target_pairs={{0,8},{8,16},{16,24},{24,32},{32,40},{40,48},{48,56},{56,64},{64,7... | collective-permute-start | bytes 331784 | tf_op jit(solution)/shard_map/while/body/eval_jaxpr/ppermute | solution.py:23
  683.4 10.8 %collective-permute-start = (f32[27,4,256]{2,0,1:T(8,128)}, f32[27,4,256]{2,0,1:T(8,128)}, u32[]{:S(2)}, u32[]{:S(2)}) collective-permute-start(f32[27,4,256]{2,0,1:T(8,128)} %get-tuple-element.258), channel_id=1, source_target_pairs={{0,8},{8,16},{16,24},{24,32},{32,40},{40,48},{48,56},{56,64},{64,7... | collective-permute-start | bytes 331784 | tf_op jit(solution)/shard_map/while/body/eval_jaxpr/ppermute | solution.py:23
  695.9 11.6 %collective-permute-start = (f32[27,4,256]{2,0,1:T(8,128)}, f32[27,4,256]{2,0,1:T(8,128)}, u32[]{:S(2)}, u32[]{:S(2)}) collective-permute-start(f32[27,4,256]{2,0,1:T(8,128)} %get-tuple-element.258), channel_id=1, source_target_pairs={{0,8},{8,16},{16,24},{24,32},{32,40},{40,48},{48,56},{56,64},{64,7... | collective-permute-start | bytes 331784 | tf_op jit(solution)/shard_map/while/body/eval_jaxpr/ppermute | solution.py:23
  709.3 10.8 %collective-permute-start = (f32[27,4,256]{2,0,1:T(8,128)}, f32[27,4,256]{2,0,1:T(8,128)}, u32[]{:S(2)}, u32[]{:S(2)}) collective-permute-start(f32[27,4,256]{2,0,1:T(8,128)} %get-tuple-element.258), channel_id=1, source_target_pairs={{0,8},{8,16},{16,24},{24,32},{32,40},{40,48},{48,56},{56,64},{64,7... | collective-permute-start | bytes 331784 | tf_op jit(solution)/shard_map/while/body/eval_jaxpr/ppermute | solution.py:23
  829.7 10.9 %collective-permute-start = (f32[27,4,256]{2,0,1:T(8,128)}, f32[27,4,256]{2,0,1:T(8,128)}, u32[]{:S(2)}, u32[]{:S(2)}) collective-permute-start(f32[27,4,256]{2,0,1:T(8,128)} %get-tuple-element.258), channel_id=1, source_target_pairs={{0,8},{8,16},{16,24},{24,32},{32,40},{40,48},{48,56},{56,64},{64,7... | collective-permute-start | bytes 331784 | tf_op jit(solution)/shard_map/while/body/eval_jaxpr/ppermute | solution.py:23
  842.4 11.5 %collective-permute-start = (f32[27,4,256]{2,0,1:T(8,128)}, f32[27,4,256]{2,0,1:T(8,128)}, u32[]{:S(2)}, u32[]{:S(2)}) collective-permute-start(f32[27,4,256]{2,0,1:T(8,128)} %get-tuple-element.258), channel_id=1, source_target_pairs={{0,8},{8,16},{16,24},{24,32},{32,40},{40,48},{48,56},{56,64},{64,7... | collective-permute-start | bytes 331784 | tf_op jit(solution)/shard_map/while/body/eval_jaxpr/ppermute | solution.py:23
  855.7 10.6 %collective-permute-start = (f32[27,4,256]{2,0,1:T(8,128)}, f32[27,4,256]{2,0,1:T(8,128)}, u32[]{:S(2)}, u32[]{:S(2)}) collective-permute-start(f32[27,4,256]{2,0,1:T(8,128)} %get-tuple-element.258), channel_id=1, source_target_pairs={{0,8},{8,16},{16,24},{24,32},{32,40},{40,48},{48,56},{56,64},{64,7... | collective-permute-start | bytes 331784 | tf_op jit(solution)/shard_map/while/body/eval_jaxpr/ppermute | solution.py:23
  (94 other events, 1039.0 us)
Sparse Core Ops, SparseCore 0:
  869.9 139.0 all-reduce.3
where the time goes:
time: 1030 us; the launch traced here: 1020 us
  waiting for transfers between devices  395 us (38%)
  local copies, waits for them, and re-layouts  298 us (29%)
  starting transfers between devices  151 us (15%)
  matrix products  149 us (14%)
  between operations  15 us (1%)
    ppermute x63, waiting for transfers between devices, passed_along(): return lax.ppermute(value, axis, pairs)  271 us
    psum x1, waiting for transfers between devices, on_device(): summed = lax.psum(accumulated, 'sp')  123 us
    ppermute x63, starting transfers between devices, passed_along(): return lax.ppermute(value, axis, pairs)  123 us
    dot_general x64, matrix products, slab_term(): lax.dot_general(flat_patch, flat_grad, (((0,), (0,)), ((), ())), preferre...  111 us
    dynamic_slice x65, local copies, waits for them, and re-layouts, slab_term(): lax.dynamic_slice_in_dim(patches, slab_number * slab_width, slab_width, 2)  95 us
    reshape x64, local copies, waits for them, and re-layouts, slab_term(): flat_patch = part_patch.reshape(cell_count, 27 * slab_width)  88.1 us
    dot_general x64, local copies, waits for them, and re-layouts, slab_term(): lax.dot_general(flat_patch, flat_grad, (((0,), (0,)), ((), ())), preferre...  87.4 us
  transfers between devices with their start and end apart: 72, of which 64 were waited for; matrix products, arithmetic and copies ran while one was open for 28% of the time, Pallas kernels for 0%

commit v1 on v0

v1 whole, which is shorter than its diff:
```python
import functools

import jax
import jax.numpy as jnp
from jax import lax
from jax.experimental import pallas as pl
from jax.experimental.pallas import tpu as pltpu
from jax.sharding import PartitionSpec as P

MESH = pl.DeviceIdType.MESH
F32 = jnp.float32
BF16 = jnp.bfloat16

LINES = 32
DEPTHS = 8


def shifted(value, by):
    width = value.shape[-2]
    rolled = pltpu.roll(value, by % width, value.ndim - 2)
    place = lax.broadcasted_iota(jnp.int32, value.shape, value.ndim - 2)
    return jnp.where(place == (0 if by == 1 else width - 1), 0.0, rolled)


def kernel(
    act_hbm, w_hbm, grad_hbm, out_ref, gin_ref, gw_ref,
    act_halo, grad_halo, w_v, act_t, act_all, grads, lhs, rhs, product, message, arrived, piece, pieces, mixed, total,
    in_sem, act_send, act_recv, g_send, g_recv, b_send, b_recv, c_send, c_recv, halo_send, halo_recv,
):
    q, s = lax.axis_index("chan"), lax.axis_index("sp")
    m, l = q // 2, q % 2
    h, c = s // 2, s % 2

    def at(line, side, depth):
        return (line * 2 + side, depth)

    barrier = pltpu.get_barrier_semaphore()

    def greet(device):
        pl.semaphore_signal(barrier, inc=1, device_id=device, device_id_type=MESH)

    n = l * 8 + s

    def greet_line(k, carry):
        peer = (n + k) % 16
        greet(at(m, peer // 8, peer % 8))
        return carry

    lax.fori_loop(1, 16, greet_line, 0)

    @pl.when(m > 0)
    def _():
        lax.fori_loop(0, DEPTHS, lambda k, t: (greet(at(m - 1, 1, k)), t)[1], 0)

    @pl.when(m < LINES - 1)
    def _():
        lax.fori_loop(0, DEPTHS, lambda k, t: (greet(at(m + 1, 0, k)), t)[1], 0)

    def greet_plane(k, carry):
        greet(at((m + k) % LINES, l, s))
        return carry

    lax.fori_loop(1, LINES, greet_plane, 0)

    own_grad = pltpu.make_async_copy(grad_hbm.at[:, 0], grad_halo.at[pl.ds(1, 2), 1], in_sem.at[0])
    own_act = pltpu.make_async_copy(act_hbm.at[:, 0], act_halo.at[pl.ds(1, 2), 1], in_sem.at[1])
    own_w = pltpu.make_async_copy(w_hbm, w_v, in_sem.at[2])
    own_grad.start()
    own_act.start()
    own_w.start()

    for halo in (act_halo, grad_halo):
        @pl.when(q == 0)
        def _(halo=halo):
            halo[:, 0] = jnp.zeros((4, 64, 256), BF16)

        @pl.when(q == 2 * LINES - 1)
        def _(halo=halo):
            halo[:, 2] = jnp.zeros((4, 64, 256), BF16)

        @pl.when(s == 0)
        def _(halo=halo):
            halo[0] = jnp.zeros((3, 64, 256), BF16)

        @pl.when(s == DEPTHS - 1)
        def _(halo=halo):
            halo[3] = jnp.zeros((3, 64, 256), BF16)

    @pl.when(m == 0)
    def _():
        act_all[0] = jnp.zeros((8, 32, 128), BF16)

    @pl.when(m == LINES - 1)
    def _():
        act_all[3] = jnp.zeros((8, 32, 128), BF16)

    position = lax.broadcasted_iota(jnp.int32, (256, 256), 0)
    channel = lax.broadcasted_iota(jnp.int32, (256, 256), 1)
    select = jnp.where(channel == (position % 32) * 8 + position // 32, 1.0, 0.0).astype(BF16)
    own_act.wait()
    turned = lax.dot_general(
        select, act_halo[1:3, 1].reshape(128, 256), (((1,), (1,)), ((), ())), preferred_element_type=F32
    )
    act_t[...] = turned.astype(BF16).reshape(8, 32, 128)
    own_grad.wait()

    has_outer = ((l == 0) & (m > 0)) | ((l == 1) & (m < LINES - 1))
    pl.semaphore_wait(barrier, 15 + LINES - 1 + jnp.where(has_outer, 16, 0))

    def grad_copy(k):
        peer = (l * 4 + h + k) % 8
        half = pl.multiple_of((peer % 4) // 2 * 128, 128)
        return pltpu.make_async_remote_copy(
            src_ref=grad_halo.at[pl.ds(1, 2), 1, :, pl.ds(half, 128)],
            dst_ref=grads.at[c, l, h],
            send_sem=g_send.at[k],
            recv_sem=g_recv.at[c],
            device_id=at(m, peer // 4, (peer % 4) * 2 + c),
            device_id_type=MESH,
        )

    def act_copy(k):
        peer = (n + k) % 16
        return pltpu.make_async_remote_copy(
            src_ref=act_t.at[(peer // 8) * 4 + peer % 4],
            dst_ref=act_all.at[1 + l, s],
            send_sem=act_send.at[k],
            recv_sem=act_recv.at[1 + l],
            device_id=at(m, peer // 8, peer % 8),
            device_id_type=MESH,
        )

    def outer_copy(k):
        peer = (n + k) % 16
        return pltpu.make_async_remote_copy(
            src_ref=act_t.at[(peer // 8) * 4 + peer % 4],
            dst_ref=act_all.at[3 - 3 * l, s],
            send_sem=act_send.at[16 + k],
            recv_sem=act_recv.at[3 - 3 * l],
            device_id=at(m - 1 + 2 * l, peer // 8, peer % 8),
            device_id_type=MESH,
        )

    own_half = pl.multiple_of(h // 2 * 128, 128)
    grad_here = pltpu.make_async_copy(
        grad_halo.at[pl.ds(1, 2), 1, :, pl.ds(own_half, 128)], grads.at[c, l, h], g_recv.at[c]
    )
    act_here = pltpu.make_async_copy(act_t.at[l * 4 + s % 4], act_all.at[1 + l, s], act_recv.at[1 + l])
    grad_here.start()
    act_here.start()

    def start(copy):
        def step(k, carry):
            copy(k).start()
            return carry
        return step

    def sent(copy):
        def step(k, carry):
            copy(k).wait_send()
            return carry
        return step

    lax.fori_loop(1, 8, start(grad_copy), 0)

    @pl.when(has_outer)
    def _():
        lax.fori_loop(0, 16, start(outer_copy), 0)

    lax.fori_loop(1, 16, start(act_copy), 0)

    pltpu.make_async_copy(grads.at[c], grads.at[c], g_recv.at[c]).wait()
    pass_on = pltpu.make_async_remote_copy(
        src_ref=grads.at[c],
        dst_ref=grads.at[c],
        send_sem=g_send.at[0],
        recv_sem=g_recv.at[c],
        device_id=(q, s + 1 - 2 * c),
        device_id_type=MESH,
    )
    pass_on.start()

    def build_rhs(core):
        def step(k, carry):
            side, depth = k // 4, k % 4
            block = grads[core, side, depth].astype(F32)
            base = pl.multiple_of((depth * 2 + core) * 256 + side * 128, 128)
            for tap, moved in enumerate((shifted(block, -1), block, shifted(block, 1))):
                rhs[pl.ds(base, 128), tap * 128 : (tap + 1) * 128] = moved.reshape(128, 128).astype(BF16)
            return carry
        lax.fori_loop(0, 8, step, 0)

    build_rhs(c)

    def halo_copies(index, halo):
        for dq in (-1, 0, 1):
            for ds in (-1, 0, 1):
                if dq == 0 and ds == 0:
                    continue
                number = index * 9 + (dq + 1) * 3 + ds + 1
                if ds == 0:
                    source, target = halo.at[pl.ds(1, 2), 1], halo.at[pl.ds(1, 2), 1 - dq]
                else:
                    source, target = halo.at[2 if ds == 1 else 1, 1], halo.at[0 if ds == 1 else 3, 1 - dq]
                there = (q + dq >= 0) & (q + dq < 2 * LINES) & (s + ds >= 0) & (s + ds < DEPTHS)
                comes = (q - dq >= 0) & (q - dq < 2 * LINES) & (s - ds >= 0) & (s - ds < DEPTHS)
                copy = functools.partial(
                    pltpu.make_async_remote_copy,
                    src_ref=source, dst_ref=target, send_sem=halo_send.at[number], recv_sem=halo_recv.at[number],
                    device_id=(q + dq, s + ds), device_id_type=MESH,
                )
                yield there, comes, copy

    both = ((0, act_halo), (1, grad_halo))
    for which in both:
        for there, _, copy in halo_copies(*which):
            pl.when(there)(lambda copy=copy: copy().start())

    for row in range(4):
        exists = (m > 0) if row == 0 else (m < LINES - 1) if row == 3 else (m >= 0)
        pl.when(exists)(pltpu.make_async_copy(act_all.at[row], act_all.at[row], act_recv.at[row]).wait)

    def build_lhs(k, carry):
        row, depth = k // 8, k % 8
        here = act_all[row, depth].astype(F32)
        before = act_all[row, jnp.maximum(depth - 1, 0)].astype(F32)
        after = act_all[row, jnp.minimum(depth + 1, DEPTHS - 1)].astype(F32)
        before = jnp.where(depth == 0, 0.0, before)
        after = jnp.where(depth == DEPTHS - 1, 0.0, after)
        low = lax.broadcasted_iota(jnp.int32, (32, 128), 1) < 64
        here_turned = pltpu.roll(here, 64, 1)
        down = jnp.where(low, pltpu.roll(before, 64, 1), here_turned).astype(BF16)
        up = jnp.where(low, here_turned, pltpu.roll(after, 64, 1)).astype(BF16)
        same = here.astype(BF16)
        for side in range(2):
            @pl.when((row - side >= 0) & (row - side < 3))
            def _(side=side):
                lanes = pl.ds(pl.multiple_of(depth * 256 + side * 128, 128), 128)
                for plane, value in enumerate((down, same, up)):
                    first = pl.multiple_of((plane * 3 + row - side) * 32, 32)
                    lhs[pl.ds(first, 32), lanes] = value
        return carry

    lax.fori_loop(0, 32, build_lhs, 0)

    pltpu.make_async_copy(grads.at[1 - c], grads.at[1 - c], g_recv.at[1 - c]).wait()
    build_rhs(1 - c)

    sums = jnp.dot(lhs[...], rhs[...], preferred_element_type=F32)
    for tap in range(3):
        product[tap] = sums[:, tap * 128 : (tap + 1) * 128]

    def build_message(k, carry):
        for tap in range(3):
            message[k, 8 * tap : 8 * tap + 8] = product[tap, pl.ds(k, 8, stride=32)]
            message[k, 24 + tap : 25 + tap] = product[tap, pl.ds(256 + k, 1)]
        return carry

    lax.fori_loop(0, LINES, build_message, 0)

    def line_copy(k):
        peer = (m + k) % LINES
        return pltpu.make_async_remote_copy(
            src_ref=message.at[peer],
            dst_ref=arrived.at[m],
            send_sem=b_send.at[k],
            recv_sem=b_recv,
            device_id=at(peer, l, s),
            device_id_type=MESH,
        )

    pltpu.make_async_copy(message.at[m], arrived.at[m], b_recv).start()
    lax.fori_loop(1, LINES, start(line_copy), 0)

    def convolve(halo, backward):
        total[...] = jnp.zeros_like(total)

        def step(k, carry):
            plane, row = k // 3, k % 3
            if backward:
                window = halo[pl.ds(2 - plane, 2), 2 - row]
            else:
                window = halo[pl.ds(plane, 2), row]
            window = window.reshape(128, 256)
            for tap in range(3):
                dims = (((1,), (1,)), ((), ())) if backward else (((1,), (0,)), ((), ()))
                total[tap] += lax.dot_general(window, w_v[k * 3 + tap], dims, preferred_element_type=F32)
            return carry

        lax.fori_loop(0, 9, step, 0)
        sums = [total[tap].reshape(2, 64, 256) for tap in range(3)]
        way = -1 if backward else 1
        return shifted(sums[0], way) + sums[1] + shifted(sums[2], -way)

    own_w.wait()
    for _, comes, copy in halo_copies(*both[0]):
        pl.when(comes)(lambda copy=copy: copy().wait_recv())
    out_ref[:, 0] = convolve(act_halo, False).astype(BF16)

    pltpu.make_async_copy(arrived, arrived, b_recv).wait()
    summed = arrived[0]
    for k in range(1, LINES):
        summed = summed + arrived[k]
    piece[...] = summed * (1.0 / 256.0)

    def depth_copy(k):
        return pltpu.make_async_remote_copy(
            src_ref=piece,
            dst_ref=pieces.at[s],
            send_sem=c_send.at[k],
            recv_sem=c_recv,
            device_id=(q, (s + k) % DEPTHS),
            device_id_type=MESH,
        )

    pltpu.make_async_copy(piece, pieces.at[s], c_recv).start()
    lax.fori_loop(1, DEPTHS, start(depth_copy), 0)

    for _, comes, copy in halo_copies(*both[1]):
        pl.when(comes)(lambda copy=copy: copy().wait_recv())
    gin_ref[:, 0] = convolve(grad_halo, True).astype(BF16)

    lax.fori_loop(1, 8, sent(grad_copy), 0)
    pass_on.wait_send()
    lax.fori_loop(1, 16, sent(act_copy), 0)

    @pl.when(has_outer)
    def _():
        lax.fori_loop(0, 16, sent(outer_copy), 0)

    for which in both:
        for there, _, copy in halo_copies(*which):
            pl.when(there)(lambda copy=copy: copy().wait_send())
    lax.fori_loop(1, LINES, sent(line_copy), 0)

    pltpu.make_async_copy(pieces, pieces, c_recv).wait()
    for depth in range(DEPTHS):
        half = depth // 4
        for tap in range(3):
            first = 4 * tap + depth % 4
            mixed[half, pl.ds(first, 8, stride=12)] = pieces[depth, 8 * tap : 8 * tap + 8]
            mixed[half, 96 + first : 97 + first] = pieces[depth, 24 + tap : 25 + tap]
    for half in range(2):
        gw_ref[:, half * 128 : (half + 1) * 128] = mixed[half]
    lax.fori_loop(1, DEPTHS, sent(depth_copy), 0)


def on_device(activations, weights, grad_output):
    vmem = pl.BlockSpec(memory_space=pltpu.VMEM)
    dma = pltpu.SemaphoreType.DMA
    output, grad_input, grad_weights = pl.pallas_call(
        kernel,
        out_shape=(
            jax.ShapeDtypeStruct((2, 1, 64, 256), BF16),
            jax.ShapeDtypeStruct((2, 1, 64, 256), BF16),
            jax.ShapeDtypeStruct((108, 256), F32),
        ),
        in_specs=[pl.BlockSpec(memory_space=pl.ANY)] * 3,
        out_specs=(vmem, vmem, vmem),
        scratch_shapes=[
            pltpu.VMEM((4, 3, 64, 256), BF16),
            pltpu.VMEM((4, 3, 64, 256), BF16),
            pltpu.VMEM((27, 256, 256), BF16),
            pltpu.VMEM((8, 32, 128), BF16),
            pltpu.VMEM((4, 8, 32, 128), BF16),
            pltpu.VMEM((2, 2, 4, 2, 64, 128), BF16),
            pltpu.VMEM((288, 2048), BF16),
            pltpu.VMEM((2048, 384), BF16),
            pltpu.VMEM((3, 288, 128), F32),
            pltpu.VMEM((LINES, 27, 128), F32),
            pltpu.VMEM((LINES, 27, 128), F32),
            pltpu.VMEM((27, 128), F32),
            pltpu.VMEM((DEPTHS, 27, 128), F32),
            pltpu.VMEM((2, 108, 128), F32),
            pltpu.VMEM((3, 128, 256), F32),
            dma((3,)),
            dma((32,)),
            dma((4,)),
            dma((8,)),
            dma((2,)),
            dma((LINES,)),
            dma(()),
            dma((DEPTHS,)),
            dma(()),
            dma((18,)),
            dma((18,)),
        ],
        compiler_params=pltpu.CompilerParams(
            collective_id=0, has_side_effects=True, vmem_limit_bytes=40 << 20
        ),
    )(activations, weights, grad_output)
    return output, grad_input, grad_weights.reshape(27, 4, 256)


def solution(mesh):
    return jax.shard_map(
        on_device,
        mesh=mesh,
        in_specs=(P("sp", "chan", None, None), P(), P("sp", "chan", None, None)),
        out_specs=(P("sp", "chan", None, None), P("sp", "chan", None, None), P(None, "chan", None)),
        check_vma=False,
    )
```

time: 1030 us -> 63.2 us (0.06); the launches traced: 1020 us -> 62.9 us
  waiting for transfers between devices: 395 us -> 0 us
  local copies, waits for them, and re-layouts: 298 us -> 5.61 us
  starting transfers between devices: 151 us -> 0 us
  matrix products: 149 us -> 0 us
  Pallas kernels: 0 us -> 56.6 us
  between operations: 15 us -> 0.65 us
    ppermute x71 -> x0, waiting for transfers between devices: 271 us -> none  [the longest x63 271 us: passed_along(): return lax.ppermute(value, axis, pairs)]
    ppermute x71 -> x0, starting transfers between devices: 151 us -> none  [the longest x63 123 us: passed_along(): return lax.ppermute(value, axis, pairs)]
    dot_general x118 -> x0, matrix products: 149 us -> none  [the longest x64 111 us: slab_term(): lax.dot_general(flat_patch, flat_grad, (((0,), (0,)), ((), ())), preferre...]
    psum x1 -> x0, waiting for transfers between devices: 123 us -> none  [on_device(): summed = lax.psum(accumulated, 'sp')]
    dynamic_slice x65 -> x0, local copies, waits for them, and re-layouts: 95 us -> none  [slab_term(): lax.dynamic_slice_in_dim(patches, slab_number * slab_width, slab_width, 2)]
    reshape x64 -> x1, local copies, waits for them, and re-layouts: 88.1 us -> 0.68 us  [on_device(): return (output, grad_input, grad_weights.reshape(27, 4, 256))]
    dot_general x64 -> x0, local copies, waits for them, and re-layouts: 87.4 us -> none  [slab_term(): lax.dot_general(flat_patch, flat_grad, (((0,), (0,)), ((), ())), preferre...]
    pallas_call x0 -> x1, Pallas kernels: none -> 56.6 us  [on_device(): pl.pallas_call(kernel, out_shape=(jax.ShapeDtypeStruct((2, 1, 64, 256), B...]
  transfers between devices with their start and end apart: 72 -> 0, of which waited for: 64 -> 0; matrix products, arithmetic and copies ran while one was open for 28% -> 0% of each run, Pallas kernels for 0% -> 0%
where the time goes in v1:
time: 63.2 us; the launch traced here: 62.9 us
  Pallas kernels  56.6 us (90%)
  local copies, waits for them, and re-layouts  5.61 us (9%)
  between operations  0.65 us (1%)
    pallas_call x1, Pallas kernels, on_device(): pl.pallas_call(kernel, out_shape=(jax.ShapeDtypeStruct((2, 1, 64, 256), B...  56.6 us
    unnamed x8, local copies, waits for them, and re-layouts  4.93 us

profile of v1, /device:TPU:1, one launch (start us, length us, event | category | flops | bytes accessed | tf_op | source)
XLA Modules:
  0.0 62.9 jit_solution(15032074429498576918)
XLA Ops:
  0.6 0.0 copy-start
  0.6 2.0 %copy-done = bf16[27,256,256]{2,1,0:T(8,128)(2,1)S(1)} copy-done((bf16[27,256,256]{2,1,0:T(8,128)(2,1)S(1)}, bf16[27,256,256]{2,1,0:T(8,128)(2,1)}, u32[]{:S(2)}) %copy-start) | copy-done | bytes 3538968
  2.6 0.0 copy-start.1
  2.6 0.8 %copy-done.1 = bf16[2,1,64,256]{3,2,1,0:T(8,128)(2,1)S(1)} copy-done((bf16[2,1,64,256]{3,2,1,0:T(8,128)(2,1)S(1)}, bf16[2,1,64,256]{3,2,1,0:T(8,128)(2,1)}, u32[]{:S(2)}) %copy-start.1) | copy-done | bytes 65560
  3.5 0.0 copy-start.2
  3.5 0.8 %copy-done.2 = bf16[2,1,64,256]{3,2,1,0:T(8,128)(2,1)S(1)} copy-done((bf16[2,1,64,256]{3,2,1,0:T(8,128)(2,1)S(1)}, bf16[2,1,64,256]{3,2,1,0:T(8,128)(2,1)}, u32[]{:S(2)}) %copy-start.2) | copy-done | bytes 65560
  4.3 56.6 %shard_map.58 = (bf16[2,1,64,256]{3,2,1,0:T(8,128)(2,1)S(1)}, bf16[2,1,64,256]{3,2,1,0:T(8,128)(2,1)S(1)}, f32[108,256]{1,0:T(8,128)S(1)}) custom-call(bf16[2,1,64,256]{3,2,1,0:T(8,128)(2,1)S(1)} %copy-done.1, bf16[27,256,256]{2,1,0:T(8,128)(2,1)S(1)} %copy-done, bf16[2,1,64,256]{3,2,1,0:T(8,128)(2,1)S(1)} %copy-done.2), custom_call_target="tpu_custom_call" | custom-call | tf_op jit(solution)/shard_map/pallas_call | solution.py:351
  60.9 0.7 %reshape.9 = f32[27,4,256]{2,1,0:T(4,128)} reshape(f32[108,256]{1,0:T(8,128)S(1)} %get-tuple-element.8) | data formatting | bytes 221184 | tf_op jit(solution)/shard_map/reshape | solution.py:392
  61.6 0.6 %copy.8 = bf16[2,1,64,256]{3,2,1,0:T(8,128)(2,1)} copy(bf16[2,1,64,256]{3,2,1,0:T(8,128)(2,1)S(1)} %get-tuple-element.12) | data formatting | bytes 131072
  62.2 0.6 %copy.9 = bf16[2,1,64,256]{3,2,1,0:T(8,128)(2,1)} copy(bf16[2,1,64,256]{3,2,1,0:T(8,128)(2,1)S(1)} %get-tuple-element.13) | data formatting | bytes 131072
Async XLA Ops:
  0.6 2.0 %copy-start = (bf16[27,256,256]{2,1,0:T(8,128)(2,1)S(1)}, bf16[27,256,256]{2,1,0:T(8,128)(2,1)}, u32[]{:S(2)}) copy-start(bf16[27,256,256]{2,1,0:T(8,128)(2,1)} %w_hbm.1) | copy-start | bytes 10616836
  2.6 0.8 %copy-start.1 = (bf16[2,1,64,256]{3,2,1,0:T(8,128)(2,1)S(1)}, bf16[2,1,64,256]{3,2,1,0:T(8,128)(2,1)}, u32[]{:S(2)}) copy-start(bf16[2,1,64,256]{3,2,1,0:T(8,128)(2,1)} %act_hbm.1) | copy-start | bytes 196612
  3.5 0.8 %copy-start.2 = (bf16[2,1,64,256]{3,2,1,0:T(8,128)(2,1)S(1)}, bf16[2,1,64,256]{3,2,1,0:T(8,128)(2,1)}, u32[]{:S(2)}) copy-start(bf16[2,1,64,256]{3,2,1,0:T(8,128)(2,1)} %grad_hbm.1) | copy-start | bytes 196612

commit v2 on v1

v2 whole, which is shorter than its diff:
```python
import functools

import jax
import jax.numpy as jnp
from jax import lax
from jax.experimental import pallas as pl
from jax.experimental.pallas import tpu as pltpu
from jax.sharding import PartitionSpec as P

MESH = pl.DeviceIdType.MESH
F32 = jnp.float32
BF16 = jnp.bfloat16

LINES = 32
DEPTHS = 8
ROW_ORDER = (1, 0, 2)


def shifted(value, by):
    width = value.shape[-2]
    rolled = pltpu.roll(value, by % width, value.ndim - 2)
    place = lax.broadcasted_iota(jnp.int32, value.shape, value.ndim - 2)
    return jnp.where(place == (0 if by == 1 else width - 1), 0.0, rolled)


def kernel(
    act_hbm, w_hbm, grad_hbm, out_ref, gin_ref, pieces,
    act_halo, grad_halo, w_v, act_t, act_all, grads, lhs, rhs, product, centre, sides, centre_in, sides_in, piece, total,
    in_sem, act_send, act_recv, g_send, g_recv, b_send, b_recv, c_send, c_recv, halo_send, halo_recv,
):
    q, s = lax.axis_index("chan"), lax.axis_index("sp")
    m, l = q // 2, q % 2
    h, c = s // 2, s % 2

    def at(line, side, depth):
        return (line * 2 + side, depth)

    own_grad = pltpu.make_async_copy(grad_hbm.at[:, 0], grad_halo.at[pl.ds(1, 2), 1], in_sem.at[0])
    own_act = pltpu.make_async_copy(act_hbm.at[:, 0], act_halo.at[pl.ds(1, 2), 1], in_sem.at[1])
    own_w = pltpu.make_async_copy(w_hbm, w_v, in_sem.at[2])
    own_grad.start()
    own_act.start()
    own_w.start()

    barrier = pltpu.get_barrier_semaphore()

    def greet(device):
        pl.semaphore_signal(barrier, inc=1, device_id=device, device_id_type=MESH)

    n = l * 8 + s

    def greet_line(k, carry):
        peer = (n + k) % 16
        greet(at(m, peer // 8, peer % 8))
        return carry

    lax.fori_loop(1, 16, greet_line, 0)

    @pl.when(m > 0)
    def _():
        lax.fori_loop(0, DEPTHS, lambda k, t: (greet(at(m - 1, 1, k)), t)[1], 0)

    @pl.when(m < LINES - 1)
    def _():
        lax.fori_loop(0, DEPTHS, lambda k, t: (greet(at(m + 1, 0, k)), t)[1], 0)

    def greet_plane(k, carry):
        greet(at((m + k) % LINES, l, s))
        return carry

    lax.fori_loop(1, LINES, greet_plane, 0)

    for halo in (act_halo, grad_halo):
        @pl.when(q == 0)
        def _(halo=halo):
            halo[1:3, 0] = jnp.zeros((2, 64, 256), BF16)

        @pl.when(q == 2 * LINES - 1)
        def _(halo=halo):
            halo[1:3, 2] = jnp.zeros((2, 64, 256), BF16)

        @pl.when(s == 0)
        def _(halo=halo):
            halo[0] = jnp.zeros((3, 64, 256), BF16)

        @pl.when(s == DEPTHS - 1)
        def _(halo=halo):
            halo[3] = jnp.zeros((3, 64, 256), BF16)

    @pl.when(m == 0)
    def _():
        act_all[0] = jnp.zeros((8, 32, 128), BF16)

    @pl.when(m == LINES - 1)
    def _():
        act_all[3] = jnp.zeros((8, 32, 128), BF16)

    position = lax.broadcasted_iota(jnp.int32, (256, 256), 0)
    channel = lax.broadcasted_iota(jnp.int32, (256, 256), 1)
    select = jnp.where(channel == (position % 32) * 8 + position // 32, 1.0, 0.0).astype(BF16)
    own_act.wait()
    turned = lax.dot_general(
        select, act_halo[1:3, 1].reshape(128, 256), (((1,), (1,)), ((), ())), preferred_element_type=F32
    )
    act_t[...] = turned.astype(BF16).reshape(8, 32, 128)
    own_grad.wait()

    has_outer = ((l == 0) & (m > 0)) | ((l == 1) & (m < LINES - 1))
    pl.semaphore_wait(barrier, 15 + LINES - 1 + jnp.where(has_outer, 16, 0))

    def halo_copy(halo, number, source, target, device):
        return functools.partial(
            pltpu.make_async_remote_copy,
            src_ref=source, dst_ref=target, send_sem=halo_send.at[number], recv_sem=halo_recv.at[number],
            device_id=device, device_id_type=MESH,
        )

    def row_copies(index, halo):
        for place, dq in enumerate((-1, 1)):
            source, target = halo.at[pl.ds(1, 2), 1], halo.at[pl.ds(1, 2), 1 - dq]
            copy = halo_copy(halo, 4 * index + place, source, target, (q + dq, s))
            yield (q + dq >= 0) & (q + dq < 2 * LINES), (q - dq >= 0) & (q - dq < 2 * LINES), copy

    def plane_copies(index, halo):
        for place, ds in enumerate((-1, 1)):
            source, target = halo.at[1 if ds == -1 else 2], halo.at[3 if ds == -1 else 0]
            copy = halo_copy(halo, 4 * index + 2 + place, source, target, (q, s + ds))
            yield (s + ds >= 0) & (s + ds < DEPTHS), (s - ds >= 0) & (s - ds < DEPTHS), copy

    both = ((0, act_halo), (1, grad_halo))

    def convolve(index, halo, planes):
        for tap in range(3):
            part = 0.0 if len(planes) == 1 else total[index, tap]
            for plane in planes:
                for row in range(3):
                    weight = w_v[(plane * 3 + row) * 3 + tap]
                    if index:
                        window, dims = halo[2 - plane : 4 - plane, 2 - row], (((1,), (1,)), ((), ()))
                    else:
                        window, dims = halo[plane : plane + 2, row], (((1,), (0,)), ((), ()))
                    part += lax.dot_general(window.reshape(128, 256), weight, dims, preferred_element_type=F32)
            total[index, tap] = part

    def joined(index):
        sums = [total[index, tap].reshape(2, 64, 256) for tap in range(3)]
        way = -1 if index else 1
        return (shifted(sums[0], way) + sums[1] + shifted(sums[2], -way)).astype(BF16)

    def grad_copy(k):
        peer = (l * 4 + h + k) % 8
        half = pl.multiple_of((peer % 4) // 2 * 128, 128)
        return pltpu.make_async_remote_copy(
            src_ref=grad_halo.at[pl.ds(1, 2), 1, :, pl.ds(half, 128)],
            dst_ref=grads.at[c, l, h],
            send_sem=g_send.at[k],
            recv_sem=g_recv.at[c],
            device_id=at(m, peer // 4, (peer % 4) * 2 + c),
            device_id_type=MESH,
        )

    def act_copy(k):
        peer = (n + k) % 16
        return pltpu.make_async_remote_copy(
            src_ref=act_t.at[(peer // 8) * 4 + peer % 4],
            dst_ref=act_all.at[1 + l, s],
            send_sem=act_send.at[k],
            recv_sem=act_recv.at[1 + l],
            device_id=at(m, peer // 8, peer % 8),
            device_id_type=MESH,
        )

    def outer_copy(k):
        peer = (n + k) % 16
        return pltpu.make_async_remote_copy(
            src_ref=act_t.at[(peer // 8) * 4 + peer % 4],
            dst_ref=act_all.at[3 - 3 * l, s],
            send_sem=act_send.at[16 + k],
            recv_sem=act_recv.at[3 - 3 * l],
            device_id=at(m - 1 + 2 * l, peer // 8, peer % 8),
            device_id_type=MESH,
        )

    own_half = pl.multiple_of(h // 2 * 128, 128)
    grad_here = pltpu.make_async_copy(
        grad_halo.at[pl.ds(1, 2), 1, :, pl.ds(own_half, 128)], grads.at[c, l, h], g_recv.at[c]
    )
    act_here = pltpu.make_async_copy(act_t.at[l * 4 + s % 4], act_all.at[1 + l, s], act_recv.at[1 + l])
    grad_here.start()
    act_here.start()

    def start(copy):
        def step(k, carry):
            copy(k).start()
            return carry
        return step

    def sent(copy):
        def step(k, carry):
            copy(k).wait_send()
            return carry
        return step

    lax.fori_loop(1, 8, start(grad_copy), 0)

    lax.fori_loop(1, 16, start(act_copy), 0)

    @pl.when(has_outer)
    def _():
        lax.fori_loop(0, 16, start(outer_copy), 0)

    pltpu.make_async_copy(grads.at[c], grads.at[c], g_recv.at[c]).wait()
    pass_on = pltpu.make_async_remote_copy(
        src_ref=grads.at[c],
        dst_ref=grads.at[c],
        send_sem=g_send.at[0],
        recv_sem=g_recv.at[c],
        device_id=(q, s + 1 - 2 * c),
        device_id_type=MESH,
    )
    pass_on.start()

    def build_rhs(core):
        for side in range(2):
            for depth in range(4):
                block = grads[core, side, depth].astype(F32)
                base = pl.multiple_of(core * 256 + depth * 512 + side * 128, 128)
                for tap, moved in enumerate((shifted(block, -1), block, shifted(block, 1))):
                    rhs[pl.ds(base, 128), tap * 128 : (tap + 1) * 128] = moved.reshape(128, 128).astype(BF16)

    build_rhs(c)

    pltpu.make_async_copy(grads.at[1 - c], grads.at[1 - c], g_recv.at[1 - c]).wait()
    build_rhs(1 - c)

    def build_lhs(row, sides):
        here = act_all[row].astype(F32)
        turned = pltpu.roll(here, 64, 2)
        nothing = jnp.zeros((1, 32, 128), F32)
        low = lax.broadcasted_iota(jnp.int32, (8, 32, 128), 2) < 64
        down = jnp.where(low, jnp.concatenate([nothing, turned[:-1]]), turned).astype(BF16)
        up = jnp.where(low, turned, jnp.concatenate([turned[1:], nothing])).astype(BF16)
        for plane, value in enumerate((down, act_all[row], up)):
            for side in sides:
                first = (ROW_ORDER.index(row - side) * 3 + plane) * 32
                for depth in range(DEPTHS):
                    lane = depth * 256 + side * 128
                    lhs[first : first + 32, lane : lane + 128] = value[depth]

    def arrival(row):
        return pltpu.make_async_copy(act_all.at[row], act_all.at[row], act_recv.at[row])

    def multiply(first, last):
        sums = jnp.dot(lhs[first:last], rhs[...], preferred_element_type=F32)
        for tap in range(3):
            product[tap, first:last] = sums[:, tap * 128 : (tap + 1) * 128]

    def line_copy(buffer, landing, number):
        def copy(k):
            peer = (m + k) % LINES
            return pltpu.make_async_remote_copy(
                src_ref=buffer.at[peer],
                dst_ref=landing.at[m],
                send_sem=b_send.at[number * LINES + k],
                recv_sem=b_recv.at[number],
                device_id=at(peer, l, s),
                device_id_type=MESH,
            )
        return copy

    centre_copy, sides_copy = line_copy(centre, centre_in, 0), line_copy(sides, sides_in, 1)

    arrival(1).wait()
    build_lhs(1, (0, 1))
    arrival(2).wait()
    build_lhs(2, (0, 1))
    multiply(0, 96)
    for k in range(LINES):
        for tap in range(3):
            centre[k, 3 * tap : 3 * tap + 3] = product[tap, pl.ds(k, 3, stride=32)]
    pltpu.make_async_copy(centre.at[m], centre_in.at[m], b_recv.at[0]).start()
    lax.fori_loop(1, LINES, start(centre_copy), 0)

    pl.when(m > 0)(arrival(0).wait)
    build_lhs(0, (0,))
    pl.when(m < LINES - 1)(arrival(3).wait)
    build_lhs(3, (1,))
    for which in both:
        for there, _, copy in row_copies(*which):
            pl.when(there)(lambda copy=copy: copy().start())
    multiply(96, 288)
    for k in range(LINES):
        for tap in range(3):
            sides[k, 6 * tap : 6 * tap + 6] = product[tap, pl.ds(96 + k, 6, stride=32)]
    pltpu.make_async_copy(sides.at[m], sides_in.at[m], b_recv.at[1]).start()
    lax.fori_loop(1, LINES, start(sides_copy), 0)

    own_w.wait()
    for which in both:
        for _, comes, copy in row_copies(*which):
            pl.when(comes)(lambda copy=copy: copy().wait_recv())
        for there, _, copy in plane_copies(*which):
            pl.when(there)(lambda copy=copy: copy().start())
    for which in both:
        convolve(*which, (1,))
    for _, comes, copy in plane_copies(*both[0]):
        pl.when(comes)(lambda copy=copy: copy().wait_recv())
    convolve(*both[0], (0, 2))
    out_ref[:, 0] = joined(0)

    pltpu.make_async_copy(centre_in, centre_in, b_recv.at[0]).wait()
    piece[0:9] = sum(centre_in[k] for k in range(LINES)) * (1.0 / 256.0)
    pltpu.make_async_copy(sides_in, sides_in, b_recv.at[1]).wait()
    piece[9:27] = sum(sides_in[k] for k in range(LINES)) * (1.0 / 256.0)

    def depth_copy(k):
        return pltpu.make_async_remote_copy(
            src_ref=piece,
            dst_ref=pieces.at[s],
            send_sem=c_send.at[k],
            recv_sem=c_recv,
            device_id=(q, (s + k) % DEPTHS),
            device_id_type=MESH,
        )

    pltpu.make_async_copy(piece, pieces.at[s], c_recv).start()
    lax.fori_loop(1, DEPTHS, start(depth_copy), 0)

    for _, comes, copy in plane_copies(*both[1]):
        pl.when(comes)(lambda copy=copy: copy().wait_recv())
    convolve(*both[1], (0, 2))
    gin_ref[:, 0] = joined(1)

    lax.fori_loop(1, 8, sent(grad_copy), 0)
    pass_on.wait_send()
    lax.fori_loop(1, 16, sent(act_copy), 0)

    @pl.when(has_outer)
    def _():
        lax.fori_loop(0, 16, sent(outer_copy), 0)

    for which in both:
        for copies in (row_copies, plane_copies):
            for there, _, copy in copies(*which):
                pl.when(there)(lambda copy=copy: copy().wait_send())
    lax.fori_loop(1, LINES, sent(centre_copy), 0)
    lax.fori_loop(1, LINES, sent(sides_copy), 0)

    pltpu.make_async_copy(pieces, pieces, c_recv).wait()
    lax.fori_loop(1, DEPTHS, sent(depth_copy), 0)


def finish(out_v, gin_v, pieces, out_hbm, gin_hbm, gw_hbm, mixed, together, sem):
    out_copy = pltpu.make_async_copy(out_v, out_hbm, sem.at[0])
    gin_copy = pltpu.make_async_copy(gin_v, gin_hbm, sem.at[1])
    out_copy.start()
    gin_copy.start()
    for depth in range(DEPTHS):
        half = depth // 4
        for tap in range(3):
            for index, row in enumerate(ROW_ORDER):
                first = (3 * row + tap) * 4 + depth % 4
                start = 6 + 6 * tap + 3 * index if index else 3 * tap
                mixed[half, pl.ds(first, 3, stride=36)] = pieces[depth, start : start + 3]
    for half in range(2):
        together[:, :, half * 128 : (half + 1) * 128] = mixed[half].reshape(27, 4, 128)
    gw_copy = pltpu.make_async_copy(together, gw_hbm, sem.at[2])
    gw_copy.start()
    out_copy.wait()
    gin_copy.wait()
    gw_copy.wait()


def on_device(activations, weights, grad_output):
    vmem = pl.BlockSpec(memory_space=pltpu.VMEM)
    dma = pltpu.SemaphoreType.DMA
    hbm = pl.BlockSpec(memory_space=pltpu.HBM)
    output, grad_input, pieces = pl.pallas_call(
        kernel,
        out_shape=(
            jax.ShapeDtypeStruct((2, 1, 64, 256), BF16),
            jax.ShapeDtypeStruct((2, 1, 64, 256), BF16),
            jax.ShapeDtypeStruct((DEPTHS, 27, 128), F32),
        ),
        in_specs=[hbm] * 3,
        out_specs=(vmem, vmem, vmem),
        scratch_shapes=[
            pltpu.VMEM((4, 3, 64, 256), BF16),
            pltpu.VMEM((4, 3, 64, 256), BF16),
            pltpu.VMEM((27, 256, 256), BF16),
            pltpu.VMEM((8, 32, 128), BF16),
            pltpu.VMEM((4, 8, 32, 128), BF16),
            pltpu.VMEM((2, 2, 4, 2, 64, 128), BF16),
            pltpu.VMEM((288, 2048), BF16),
            pltpu.VMEM((2048, 384), BF16),
            pltpu.VMEM((3, 288, 128), F32),
            pltpu.VMEM((LINES, 9, 128), F32),
            pltpu.VMEM((LINES, 18, 128), F32),
            pltpu.VMEM((LINES, 9, 128), F32),
            pltpu.VMEM((LINES, 18, 128), F32),
            pltpu.VMEM((27, 128), F32),
            pltpu.VMEM((2, 3, 128, 256), F32),
            dma((3,)),
            dma((32,)),
            dma((4,)),
            dma((8,)),
            dma((2,)),
            dma((2 * LINES,)),
            dma((2,)),
            dma((DEPTHS,)),
            dma(()),
            dma((8,)),
            dma((8,)),
        ],
        compiler_params=pltpu.CompilerParams(
            collective_id=0, has_side_effects=True, vmem_limit_bytes=40 << 20
        ),
    )(*(pltpu.with_memory_space_constraint(operand, pltpu.HBM) for operand in (activations, weights, grad_output)))
    return pl.pallas_call(
        finish,
        out_shape=(
            jax.ShapeDtypeStruct((2, 1, 64, 256), BF16),
            jax.ShapeDtypeStruct((2, 1, 64, 256), BF16),
            jax.ShapeDtypeStruct((27, 4, 256), F32),
        ),
        in_specs=[vmem] * 3,
        out_specs=(hbm, hbm, hbm),
        scratch_shapes=[pltpu.VMEM((2, 108, 128), F32), pltpu.VMEM((27, 4, 256), F32), dma((3,))],
        compiler_params=pltpu.CompilerParams(vmem_limit_bytes=8 << 20),
    )(output, grad_input, pieces)


def solution(mesh):
    return jax.shard_map(
        on_device,
        mesh=mesh,
        in_specs=(P("sp", "chan", None, None), P(), P("sp", "chan", None, None)),
        out_specs=(P("sp", "chan", None, None), P("sp", "chan", None, None), P(None, "chan", None)),
        check_vma=False,
    )
```

time: 63.2 us -> 54.2 us (0.86)
  local copies, waits for them, and re-layouts: 5.61 us -> 0 us
  Pallas kernels: 56.6 us -> 53.5 us
    unnamed x8 -> x0, local copies, waits for them, and re-layouts: 4.93 us -> none
    pallas_call x1, Pallas kernels: 56.6 us -> 52.7 us  [on_device(): pl.pallas_call(kernel, out_shape=(jax.ShapeDtypeStruct((2, 1, 64, 256), B...]
    pallas_call x0 -> x1, Pallas kernels: none -> 0.72 us  [on_device(): pl.pallas_call(finish, out_shape=(jax.ShapeDtypeStruct((2, 1, 64, 256), B...]
    reshape x1 -> x0, local copies, waits for them, and re-layouts: 0.68 us -> none  [on_device(): return (output, grad_input, grad_weights.reshape(27, 4, 256))]
where the time goes in v2:
time: 54.2 us; the launch traced here: 54.1 us
  Pallas kernels  53.5 us (99%)
  between operations  0.64 us (1%)
    pallas_call x1, Pallas kernels, on_device(): pl.pallas_call(kernel, out_shape=(jax.ShapeDtypeStruct((2, 1, 64, 256), B...  52.7 us

profile of v2, /device:TPU:1, one launch (start us, length us, event | category | flops | bytes accessed | tf_op | source)
XLA Modules:
  0.0 54.1 jit_solution(3825703231491709275)
XLA Ops:
  0.6 52.7 %shard_map.58 = (bf16[2,1,64,256]{3,2,1,0:T(8,128)(2,1)S(1)}, bf16[2,1,64,256]{3,2,1,0:T(8,128)(2,1)S(1)}, f32[8,27,128]{2,1,0:T(8,128)S(1)}) custom-call(bf16[2,1,64,256]{3,2,1,0:T(8,128)(2,1)} %act_hbm.1, bf16[27,256,256]{2,1,0:T(8,128)(2,1)} %w_hbm.1, bf16[2,1,64,256]{3,2,1,0:T(8,128)(2,1)} %grad_hbm.1), custom_call_target="tpu_custom_call" | custom-call | tf_op jit(solution)/shard_map/pallas_call | solution.py:378
  53.4 0.7 %shard_map.59 = (bf16[2,1,64,256]{3,2,1,0:T(8,128)(2,1)}, bf16[2,1,64,256]{3,2,1,0:T(8,128)(2,1)}, f32[27,4,256]{2,1,0:T(4,128)}) custom-call(bf16[2,1,64,256]{3,2,1,0:T(8,128)(2,1)S(1)} %get-tuple-element.6.out_v, bf16[2,1,64,256]{3,2,1,0:T(8,128)(2,1)S(1)} %get-tuple-element.7.gin_v, f32[8,27,128]{2,1,0:T(8,128)S(1)} %get-tuple-element.8.pieces), custom_call_target="tpu_custom_call" | custom-call | tf_op jit(solution)/shard_map/pallas_call | solution.py:419

commit v3 on v2

--- a/solution.py
+++ b/solution.py
@@ -24,16 +24,21 @@
 
 
 def kernel(
-    act_hbm, w_hbm, grad_hbm, out_ref, gin_ref, pieces,
-    act_halo, grad_halo, w_v, act_t, act_all, grads, lhs, rhs, product, centre, sides, centre_in, sides_in, piece, total,
+    act_hbm, w_hbm, grad_hbm, out_ref, gin_ref, centre_out, sides_out,
+    act_halo, grad_halo, w_v, act_t, act_all, grads, lhs, rhs, product, centre, sides, centre_in, sides_in, centre_sum, sides_sum, total,
     in_sem, act_send, act_recv, g_send, g_recv, b_send, b_recv, c_send, c_recv, halo_send, halo_recv,
 ):
     q, s = lax.axis_index("chan"), lax.axis_index("sp")
     m, l = q // 2, q % 2
     h, c = s // 2, s % 2
 
+    z = 2 * h + l
+
     def at(line, side, depth):
         return (line * 2 + side, depth)
+
+    def away(k, count):
+        return count // 2 + jnp.where(k % 2 == 0, k // 2, -((k + 1) // 2))
 
     own_grad = pltpu.make_async_copy(grad_hbm.at[:, 0], grad_halo.at[pl.ds(1, 2), 1], in_sem.at[0])
     own_act = pltpu.make_async_copy(act_hbm.at[:, 0], act_halo.at[pl.ds(1, 2), 1], in_sem.at[1])
@@ -103,8 +108,6 @@
         select, act_halo[1:3, 1].reshape(128, 256), (((1,), (1,)), ((), ())), preferred_element_type=F32
     )
     act_t[...] = turned.astype(BF16).reshape(8, 32, 128)
-    own_grad.wait()
-
     has_outer = ((l == 0) & (m > 0)) | ((l == 1) & (m < LINES - 1))
     pl.semaphore_wait(barrier, 15 + LINES - 1 + jnp.where(has_outer, 16, 0))
 
@@ -148,46 +151,49 @@
         return (shifted(sums[0], way) + sums[1] + shifted(sums[2], -way)).astype(BF16)
 
     def grad_copy(k):
-        peer = (l * 4 + h + k) % 8
-        half = pl.multiple_of((peer % 4) // 2 * 128, 128)
+        there = (z + away(k, 8)) % 8
+        half = pl.multiple_of(there // 4 * 128, 128)
         return pltpu.make_async_remote_copy(
-            src_ref=grad_halo.at[pl.ds(1, 2), 1, :, pl.ds(half, 128)],
+            src_ref=grad_hbm.at[:, 0, :, pl.ds(half, 128)],
             dst_ref=grads.at[c, l, h],
             send_sem=g_send.at[k],
             recv_sem=g_recv.at[c],
-            device_id=at(m, peer // 4, (peer % 4) * 2 + c),
+            device_id=at(m, there % 2, there // 2 * 2 + c),
             device_id_type=MESH,
         )
 
+    def in_line(k):
+        there = (z + away(k // 2, 8)) % 8
+        return there % 2, there // 2 * 2 + (c + 1 + k) % 2
+
     def act_copy(k):
-        peer = (n + k) % 16
+        side, depth = in_line(k)
         return pltpu.make_async_remote_copy(
-            src_ref=act_t.at[(peer // 8) * 4 + peer % 4],
+            src_ref=act_t.at[side * 4 + depth % 4],
             dst_ref=act_all.at[1 + l, s],
             send_sem=act_send.at[k],
             recv_sem=act_recv.at[1 + l],
-            device_id=at(m, peer // 8, peer % 8),
+            device_id=at(m, side, depth),
             device_id_type=MESH,
         )
 
     def outer_copy(k):
-        peer = (n + k) % 16
+        side, depth = in_line(k)
         return pltpu.make_async_remote_copy(
-            src_ref=act_t.at[(peer // 8) * 4 + peer % 4],
+            src_ref=act_t.at[side * 4 + depth % 4],
             dst_ref=act_all.at[3 - 3 * l, s],
             send_sem=act_send.at[16 + k],
             recv_sem=act_recv.at[3 - 3 * l],
-            device_id=at(m - 1 + 2 * l, peer // 8, peer % 8),
+            device_id=at(m - 1 + 2 * l, side, depth),
             device_id_type=MESH,
         )
 
     own_half = pl.multiple_of(h // 2 * 128, 128)
     grad_here = pltpu.make_async_copy(
-        grad_halo.at[pl.ds(1, 2), 1, :, pl.ds(own_half, 128)], grads.at[c, l, h], g_recv.at[c]
+        grad_hbm.at[:, 0, :, pl.ds(own_half, 128)], grads.at[c, l, h], g_recv.at[c]
     )
     act_here = pltpu.make_async_copy(act_t.at[l * 4 + s % 4], act_all.at[1 + l, s], act_recv.at[1 + l])
     grad_here.start()
-    act_here.start()
 
     def start(copy):
         def step(k, carry):
@@ -201,9 +207,10 @@
             return carry
         return step
 
-    lax.fori_loop(1, 8, start(grad_copy), 0)
-
-    lax.fori_loop(1, 16, start(act_copy), 0)
+    lax.fori_loop(0, 7, start(grad_copy), 0)
+
+    act_here.start()
+    lax.fori_loop(0, 15, start(act_copy), 0)
 
     @pl.when(has_outer)
     def _():
@@ -213,7 +220,7 @@
     pass_on = pltpu.make_async_remote_copy(
         src_ref=grads.at[c],
         dst_ref=grads.at[c],
-        send_sem=g_send.at[0],
+        send_sem=g_send.at[7],
         recv_sem=g_recv.at[c],
         device_id=(q, s + 1 - 2 * c),
         device_id_type=MESH,
@@ -224,7 +231,7 @@
         for side in range(2):
             for depth in range(4):
                 block = grads[core, side, depth].astype(F32)
-                base = pl.multiple_of(core * 256 + depth * 512 + side * 128, 128)
+                base = pl.multiple_of(core * 128 + depth * 256 + side * 1024, 128)
                 for tap, moved in enumerate((shifted(block, -1), block, shifted(block, 1))):
                     rhs[pl.ds(base, 128), tap * 128 : (tap + 1) * 128] = moved.reshape(128, 128).astype(BF16)
 
@@ -244,20 +251,19 @@
             for side in sides:
                 first = (ROW_ORDER.index(row - side) * 3 + plane) * 32
                 for depth in range(DEPTHS):
-                    lane = depth * 256 + side * 128
+                    lane = depth * 128 + side * 1024
                     lhs[first : first + 32, lane : lane + 128] = value[depth]
 
     def arrival(row):
         return pltpu.make_async_copy(act_all.at[row], act_all.at[row], act_recv.at[row])
 
-    def multiply(first, last):
-        sums = jnp.dot(lhs[first:last], rhs[...], preferred_element_type=F32)
-        for tap in range(3):
-            product[tap, first:last] = sums[:, tap * 128 : (tap + 1) * 128]
+    def multiply(rows, cells):
+        sums = jnp.dot(lhs[rows, cells], rhs[cells], preferred_element_type=F32)
+        return [sums[:, tap * 128 : (tap + 1) * 128] for tap in range(3)]
 
     def line_copy(buffer, landing, number):
         def copy(k):
-            peer = (m + k) % LINES
+            peer = (m // 8 + away(k % 4, 4)) % 4 * 8 + (m + away(k // 4, 8)) % 8
             return pltpu.make_async_remote_copy(
                 src_ref=buffer.at[peer],
                 dst_ref=landing.at[m],
@@ -270,30 +276,41 @@
 
     centre_copy, sides_copy = line_copy(centre, centre_in, 0), line_copy(sides, sides_in, 1)
 
+    own_grad.wait()
+    for which in both:
+        for there, _, copy in row_copies(*which):
+            pl.when(there)(lambda copy=copy: copy().start())
+
     arrival(1).wait()
     build_lhs(1, (0, 1))
     arrival(2).wait()
     build_lhs(2, (0, 1))
-    multiply(0, 96)
+    for tap, part in enumerate(multiply(slice(0, 96), slice(None))):
+        product[tap, 0:96] = part
     for k in range(LINES):
         for tap in range(3):
             centre[k, 3 * tap : 3 * tap + 3] = product[tap, pl.ds(k, 3, stride=32)]
     pltpu.make_async_copy(centre.at[m], centre_in.at[m], b_recv.at[0]).start()
-    lax.fori_loop(1, LINES, start(centre_copy), 0)
-
+    lax.fori_loop(0, LINES - 1, start(centre_copy), 0)
+
+    low_cells, high_cells = slice(0, 1024), slice(1024, 2048)
+    for tap, part in enumerate(multiply(slice(96, 192), high_cells)):
+        product[tap, 96:192] = part
+    for tap, part in enumerate(multiply(slice(192, 288), low_cells)):
+        product[tap, 192:288] = part
     pl.when(m > 0)(arrival(0).wait)
     build_lhs(0, (0,))
     pl.when(m < LINES - 1)(arrival(3).wait)
     build_lhs(3, (1,))
-    for which in both:
-        for there, _, copy in row_copies(*which):
-            pl.when(there)(lambda copy=copy: copy().start())
-    multiply(96, 288)
+    for tap, part in enumerate(multiply(slice(96, 192), low_cells)):
+        product[tap, 96:192] += part
+    for tap, part in enumerate(multiply(slice(192, 288), high_cells)):
+        product[tap, 192:288] += part
     for k in range(LINES):
         for tap in range(3):
             sides[k, 6 * tap : 6 * tap + 6] = product[tap, pl.ds(96 + k, 6, stride=32)]
     pltpu.make_async_copy(sides.at[m], sides_in.at[m], b_recv.at[1]).start()
-    lax.fori_loop(1, LINES, start(sides_copy), 0)
+    lax.fori_loop(0, LINES - 1, start(sides_copy), 0)
 
     own_w.wait()
     for which in both:
@@ -308,32 +325,37 @@
     convolve(*both[0], (0, 2))
     out_ref[:, 0] = joined(0)
 
-    pltpu.make_async_copy(centre_in, centre_in, b_recv.at[0]).wait()
-    piece[0:9] = sum(centre_in[k] for k in range(LINES)) * (1.0 / 256.0)
-    pltpu.make_async_copy(sides_in, sides_in, b_recv.at[1]).wait()
-    piece[9:27] = sum(sides_in[k] for k in range(LINES)) * (1.0 / 256.0)
-
-    def depth_copy(k):
-        return pltpu.make_async_remote_copy(
-            src_ref=piece,
-            dst_ref=pieces.at[s],
-            send_sem=c_send.at[k],
-            recv_sem=c_recv,
-            device_id=(q, (s + k) % DEPTHS),
-            device_id_type=MESH,
-        )
-
-    pltpu.make_async_copy(piece, pieces.at[s], c_recv).start()
-    lax.fori_loop(1, DEPTHS, start(depth_copy), 0)
+    def depth_copy(mine, landing, number):
+        def copy(k):
+            there = (h + away(k // 2, 4)) % 4
+            return pltpu.make_async_remote_copy(
+                src_ref=mine,
+                dst_ref=landing.at[s],
+                send_sem=c_send.at[number * DEPTHS + k],
+                recv_sem=c_recv.at[number],
+                device_id=(q, there * 2 + (c + 1 + k) % 2),
+                device_id_type=MESH,
+            )
+        return copy
+
+    gathers = []
+    for number, (summands, mine, landing) in enumerate(
+        ((centre_in, centre_sum, centre_out), (sides_in, sides_sum, sides_out))
+    ):
+        pltpu.make_async_copy(summands, summands, b_recv.at[number]).wait()
+        mine[...] = sum(summands[k] for k in range(LINES)) * (1.0 / 256.0)
+        pltpu.make_async_copy(mine, landing.at[s], c_recv.at[number]).start()
+        gathers.append(depth_copy(mine, landing, number))
+        lax.fori_loop(0, DEPTHS - 1, start(gathers[number]), 0)
 
     for _, comes, copy in plane_copies(*both[1]):
         pl.when(comes)(lambda copy=copy: copy().wait_recv())
     convolve(*both[1], (0, 2))
     gin_ref[:, 0] = joined(1)
 
-    lax.fori_loop(1, 8, sent(grad_copy), 0)
+    lax.fori_loop(0, 7, sent(grad_copy), 0)
     pass_on.wait_send()
-    lax.fori_loop(1, 16, sent(act_copy), 0)
+    lax.fori_loop(0, 15, sent(act_copy), 0)
 
     @pl.when(has_outer)
     def _():
@@ -343,14 +365,15 @@
         for copies in (row_copies, plane_copies):
             for there, _, copy in copies(*which):
                 pl.when(there)(lambda copy=copy: copy().wait_send())
-    lax.fori_loop(1, LINES, sent(centre_copy), 0)
-    lax.fori_loop(1, LINES, sent(sides_copy), 0)
-
-    pltpu.make_async_copy(pieces, pieces, c_recv).wait()
-    lax.fori_loop(1, DEPTHS, sent(depth_copy), 0)
-
-
-def finish(out_v, gin_v, pieces, out_hbm, gin_hbm, gw_hbm, mixed, together, sem):
+    lax.fori_loop(0, LINES - 1, sent(centre_copy), 0)
+    lax.fori_loop(0, LINES - 1, sent(sides_copy), 0)
+
+    for number, landing in enumerate((centre_out, sides_out)):
+        pltpu.make_async_copy(landing, landing, c_recv.at[number]).wait()
+        lax.fori_loop(0, DEPTHS - 1, sent(gathers[number]), 0)
+
+
+def finish(out_v, gin_v, centre, sides, out_hbm, gin_hbm, gw_hbm, mixed, together, sem):
     out_copy = pltpu.make_async_copy(out_v, out_hbm, sem.at[0])
     gin_copy = pltpu.make_async_copy(gin_v, gin_hbm, sem.at[1])
     out_copy.start()
@@ -360,8 +383,8 @@
         for tap in range(3):
             for index, row in enumerate(ROW_ORDER):
                 first = (3 * row + tap) * 4 + depth % 4
-                start = 6 + 6 * tap + 3 * index if index else 3 * tap
-                mixed[half, pl.ds(first, 3, stride=36)] = pieces[depth, start : start + 3]
+                start = 6 * tap + 3 * index - 3 if index else 3 * tap
+                mixed[half, pl.ds(first, 3, stride=36)] = (sides if index else centre)[depth, start : start + 3]
     for half in range(2):
         together[:, :, half * 128 : (half + 1) * 128] = mixed[half].reshape(27, 4, 128)
     gw_copy = pltpu.make_async_copy(together, gw_hbm, sem.at[2])
@@ -375,15 +398,16 @@
     vmem = pl.BlockSpec(memory_space=pltpu.VMEM)
     dma = pltpu.SemaphoreType.DMA
     hbm = pl.BlockSpec(memory_space=pltpu.HBM)
-    output, grad_input, pieces = pl.pallas_call(
+    results = pl.pallas_call(
         kernel,
         out_shape=(
             jax.ShapeDtypeStruct((2, 1, 64, 256), BF16),
             jax.ShapeDtypeStruct((2, 1, 64, 256), BF16),
-            jax.ShapeDtypeStruct((DEPTHS, 27, 128), F32),
+            jax.ShapeDtypeStruct((DEPTHS, 9, 128), F32),
+            jax.ShapeDtypeStruct((DEPTHS, 18, 128), F32),
         ),
         in_specs=[hbm] * 3,
-        out_specs=(vmem, vmem, vmem),
+        out_specs=(vmem,) * 4,
         scratch_shapes=[
             pltpu.VMEM((4, 3, 64, 256), BF16),
             pltpu.VMEM((4, 3, 64, 256), BF16),
@@ -398,7 +422,8 @@
             pltpu.VMEM((LINES, 18, 128), F32),
             pltpu.VMEM((LINES, 9, 128), F32),
             pltpu.VMEM((LINES, 18, 128), F32),
-            pltpu.VMEM((27, 128), F32),
+            pltpu.VMEM((9, 128), F32),
+            pltpu.VMEM((18, 128), F32),
             pltpu.VMEM((2, 3, 128, 256), F32),
             dma((3,)),
             dma((32,)),
@@ -407,8 +432,8 @@
             dma((2,)),
             dma((2 * LINES,)),
             dma((2,)),
-            dma((DEPTHS,)),
-            dma(()),
+            dma((2 * DEPTHS,)),
+            dma((2,)),
             dma((8,)),
             dma((8,)),
         ],
@@ -423,11 +448,11 @@
             jax.ShapeDtypeStruct((2, 1, 64, 256), BF16),
             jax.ShapeDtypeStruct((27, 4, 256), F32),
         ),
-        in_specs=[vmem] * 3,
+        in_specs=[vmem] * 4,
         out_specs=(hbm, hbm, hbm),
         scratch_shapes=[pltpu.VMEM((2, 108, 128), F32), pltpu.VMEM((27, 4, 256), F32), dma((3,))],
         compiler_params=pltpu.CompilerParams(vmem_limit_bytes=8 << 20),
-    )(output, grad_input, pieces)
+    )(*results)
 
 
 def solution(mesh):

time: 54.2 us -> 50.9 us (0.939)
  Pallas kernels: 53.5 us -> 50.1 us
    pallas_call x1, Pallas kernels: 52.7 us -> 49.4 us  [on_device(): pl.pallas_call(kernel, out_shape=(jax.ShapeDtypeStruct((2, 1, 64, 256), B...]
where the time goes in v3:
time: 50.9 us; the launch traced here: 50.8 us
  Pallas kernels  50.1 us (98%)
  between operations  0.64 us (1%)
    pallas_call x1, Pallas kernels, on_device(): pl.pallas_call(kernel, out_shape=(jax.ShapeDtypeStruct((2, 1, 64, 256), B...  49.4 us

profile of v3, /device:TPU:1, one launch (start us, length us, event | category | flops | bytes accessed | tf_op | source)
XLA Modules:
  0.0 50.8 jit_solution(8690558278718857053)
XLA Ops:
  0.6 49.4 %shard_map.58 = (bf16[2,1,64,256]{3,2,1,0:T(8,128)(2,1)S(1)}, bf16[2,1,64,256]{3,2,1,0:T(8,128)(2,1)S(1)}, f32[8,9,128]{2,1,0:T(8,128)S(1)}, f32[8,18,128]{2,1,0:T(8,128)S(1)}) custom-call(bf16[2,1,64,256]{3,2,1,0:T(8,128)(2,1)} %act_hbm.1, bf16[27,256,256]{2,1,0:T(8,128)(2,1)} %w_hbm.1, bf16[2,1,64,256]{3,2,1,0:T(8,128)(2,1)} %grad_hbm.1), custom_call_target="tpu_custom_call" | custom-call | tf_op jit(solution)/shard_map/pallas_call | solution.py:401
  50.0 0.7 %shard_map.59 = (bf16[2,1,64,256]{3,2,1,0:T(8,128)(2,1)}, bf16[2,1,64,256]{3,2,1,0:T(8,128)(2,1)}, f32[27,4,256]{2,1,0:T(4,128)}) custom-call(bf16[2,1,64,256]{3,2,1,0:T(8,128)(2,1)S(1)} %get-tuple-element.7.out_v, bf16[2,1,64,256]{3,2,1,0:T(8,128)(2,1)S(1)} %get-tuple-element.8.gin_v, f32[8,9,128]{2,1,0:T(8,128)S(1)} %get-tuple-element.9.centre, ...), custom_call_target="tpu_custom_call" | custom-call | tf_op jit(solution)/shard_map/pallas_call | solution.py:444

commit v4 on v3

--- a/solution.py
+++ b/solution.py
@@ -47,6 +47,8 @@
     own_act.start()
     own_w.start()
 
+    has_outer = ((l == 0) & (m > 0)) | ((l == 1) & (m < LINES - 1))
+
     barrier = pltpu.get_barrier_semaphore()
 
     def greet(device):
@@ -61,13 +63,9 @@
 
     lax.fori_loop(1, 16, greet_line, 0)
 
-    @pl.when(m > 0)
+    @pl.when(has_outer)
     def _():
-        lax.fori_loop(0, DEPTHS, lambda k, t: (greet(at(m - 1, 1, k)), t)[1], 0)
-
-    @pl.when(m < LINES - 1)
-    def _():
-        lax.fori_loop(0, DEPTHS, lambda k, t: (greet(at(m + 1, 0, k)), t)[1], 0)
+        greet(at(m - 1 + 2 * l, 1 - l, s))
 
     def greet_plane(k, carry):
         greet(at((m + k) % LINES, l, s))
@@ -108,8 +106,7 @@
         select, act_halo[1:3, 1].reshape(128, 256), (((1,), (1,)), ((), ())), preferred_element_type=F32
     )
     act_t[...] = turned.astype(BF16).reshape(8, 32, 128)
-    has_outer = ((l == 0) & (m > 0)) | ((l == 1) & (m < LINES - 1))
-    pl.semaphore_wait(barrier, 15 + LINES - 1 + jnp.where(has_outer, 16, 0))
+    pl.semaphore_wait(barrier, 15 + LINES - 1 + jnp.where(has_outer, 1, 0))
 
     def halo_copy(halo, number, source, target, device):
         return functools.partial(
@@ -177,16 +174,17 @@
             device_id_type=MESH,
         )
 
-    def outer_copy(k):
-        side, depth = in_line(k)
+    def outer_copy(row, way):
         return pltpu.make_async_remote_copy(
-            src_ref=act_t.at[side * 4 + depth % 4],
-            dst_ref=act_all.at[3 - 3 * l, s],
-            send_sem=act_send.at[16 + k],
-            recv_sem=act_recv.at[3 - 3 * l],
-            device_id=at(m - 1 + 2 * l, side, depth),
+            src_ref=act_all.at[row],
+            dst_ref=act_all.at[row - 2 * way],
+            send_sem=act_send.at[15 + row],
+            recv_sem=act_recv.at[row - 2 * way],
+            device_id=at(m + way, l, s),
             device_id_type=MESH,
         )
+
+    up, down = outer_copy(2, 1), outer_copy(1, -1)
 
     own_half = pl.multiple_of(h // 2 * 128, 128)
     grad_here = pltpu.make_async_copy(
@@ -207,38 +205,10 @@
             return carry
         return step
 
-    lax.fori_loop(0, 7, start(grad_copy), 0)
-
     act_here.start()
     lax.fori_loop(0, 15, start(act_copy), 0)
 
-    @pl.when(has_outer)
-    def _():
-        lax.fori_loop(0, 16, start(outer_copy), 0)
-
-    pltpu.make_async_copy(grads.at[c], grads.at[c], g_recv.at[c]).wait()
-    pass_on = pltpu.make_async_remote_copy(
-        src_ref=grads.at[c],
-        dst_ref=grads.at[c],
-        send_sem=g_send.at[7],
-        recv_sem=g_recv.at[c],
-        device_id=(q, s + 1 - 2 * c),
-        device_id_type=MESH,
-    )
-    pass_on.start()
-
-    def build_rhs(core):
-        for side in range(2):
-            for depth in range(4):
-                block = grads[core, side, depth].astype(F32)
-                base = pl.multiple_of(core * 128 + depth * 256 + side * 1024, 128)
-                for tap, moved in enumerate((shifted(block, -1), block, shifted(block, 1))):
-                    rhs[pl.ds(base, 128), tap * 128 : (tap + 1) * 128] = moved.reshape(128, 128).astype(BF16)
-
-    build_rhs(c)
-
-    pltpu.make_async_copy(grads.at[1 - c], grads.at[1 - c], g_recv.at[1 - c]).wait()
-    build_rhs(1 - c)
+    lax.fori_loop(0, 7, start(grad_copy), 0)
 
     def build_lhs(row, sides):
         here = act_all[row].astype(F32)
@@ -251,15 +221,59 @@
             for side in sides:
                 first = (ROW_ORDER.index(row - side) * 3 + plane) * 32
                 for depth in range(DEPTHS):
-                    lane = depth * 128 + side * 1024
+                    lane = depth % 2 * 1024 + side * 512 + depth // 2 * 128
                     lhs[first : first + 32, lane : lane + 128] = value[depth]
 
     def arrival(row):
         return pltpu.make_async_copy(act_all.at[row], act_all.at[row], act_recv.at[row])
 
-    def multiply(rows, cells):
+    arrival(1).wait()
+    pl.when(m > 0)(down.start)
+    arrival(2).wait()
+    pl.when(m < LINES - 1)(up.start)
+    build_lhs(1, (0, 1))
+    build_lhs(2, (0, 1))
+    pltpu.make_async_copy(grads.at[c], grads.at[c], g_recv.at[c]).wait()
+    pass_on = pltpu.make_async_remote_copy(
+        src_ref=grads.at[c],
+        dst_ref=grads.at[c],
+        send_sem=g_send.at[7],
+        recv_sem=g_recv.at[c],
+        device_id=(q, s + 1 - 2 * c),
+        device_id_type=MESH,
+    )
+    pass_on.start()
+    own_grad.wait()
+    for which in both:
+        for there, _, copy in row_copies(*which):
+            pl.when(there)(lambda copy=copy: copy().start())
+
+    def build_rhs(core):
+        for side in range(2):
+            for depth in range(4):
+                block = grads[core, side, depth].astype(F32)
+                base = pl.multiple_of(core * 1024 + side * 512 + depth * 128, 128)
+                for tap, moved in enumerate((shifted(block, -1), block, shifted(block, 1))):
+                    rhs[pl.ds(base, 128), tap * 128 : (tap + 1) * 128] = moved.reshape(128, 128).astype(BF16)
+
+    build_rhs(c)
+
+    def multiply(rows, core, first):
+        cells = pl.ds(pl.multiple_of(core * 1024, 1024), 1024)
         sums = jnp.dot(lhs[rows, cells], rhs[cells], preferred_element_type=F32)
-        return [sums[:, tap * 128 : (tap + 1) * 128] for tap in range(3)]
+        for tap in range(3):
+            part = sums[:, tap * 128 : (tap + 1) * 128]
+            product[tap, rows] = part if first else product[tap, rows] + part
+
+    centre_rows, side_rows = slice(0, 96), slice(96, 288)
+    multiply(centre_rows, c, True)
+    pl.when(m > 0)(arrival(0).wait)
+    build_lhs(0, (0,))
+    pl.when(m < LINES - 1)(arrival(3).wait)
+    build_lhs(3, (1,))
+    multiply(side_rows, c, True)
+    pltpu.make_async_copy(grads.at[1 - c], grads.at[1 - c], g_recv.at[1 - c]).wait()
+    build_rhs(1 - c)
 
     def line_copy(buffer, landing, number):
         def copy(k):
@@ -276,36 +290,15 @@
 
     centre_copy, sides_copy = line_copy(centre, centre_in, 0), line_copy(sides, sides_in, 1)
 
-    own_grad.wait()
-    for which in both:
-        for there, _, copy in row_copies(*which):
-            pl.when(there)(lambda copy=copy: copy().start())
-
-    arrival(1).wait()
-    build_lhs(1, (0, 1))
-    arrival(2).wait()
-    build_lhs(2, (0, 1))
-    for tap, part in enumerate(multiply(slice(0, 96), slice(None))):
-        product[tap, 0:96] = part
+
+    multiply(centre_rows, 1 - c, False)
     for k in range(LINES):
         for tap in range(3):
             centre[k, 3 * tap : 3 * tap + 3] = product[tap, pl.ds(k, 3, stride=32)]
     pltpu.make_async_copy(centre.at[m], centre_in.at[m], b_recv.at[0]).start()
     lax.fori_loop(0, LINES - 1, start(centre_copy), 0)
 
-    low_cells, high_cells = slice(0, 1024), slice(1024, 2048)
-    for tap, part in enumerate(multiply(slice(96, 192), high_cells)):
-        product[tap, 96:192] = part
-    for tap, part in enumerate(multiply(slice(192, 288), low_cells)):
-        product[tap, 192:288] = part
-    pl.when(m > 0)(arrival(0).wait)
-    build_lhs(0, (0,))
-    pl.when(m < LINES - 1)(arrival(3).wait)
-    build_lhs(3, (1,))
-    for tap, part in enumerate(multiply(slice(96, 192), low_cells)):
-        product[tap, 96:192] += part
-    for tap, part in enumerate(multiply(slice(192, 288), high_cells)):
-        product[tap, 192:288] += part
+    multiply(side_rows, 1 - c, False)
     for k in range(LINES):
         for tap in range(3):
             sides[k, 6 * tap : 6 * tap + 6] = product[tap, pl.ds(96 + k, 6, stride=32)]
@@ -357,9 +350,8 @@
     pass_on.wait_send()
     lax.fori_loop(0, 15, sent(act_copy), 0)
 
-    @pl.when(has_outer)
-    def _():
-        lax.fori_loop(0, 16, sent(outer_copy), 0)
+    pl.when(m < LINES - 1)(up.wait_send)
+    pl.when(m > 0)(down.wait_send)
 
     for which in both:
         for copies in (row_copies, plane_copies):

time: 50.9 us -> 49.1 us (0.965)
  Pallas kernels: 50.1 us -> 48.4 us
    pallas_call x1, Pallas kernels: 49.4 us -> 47.6 us  [on_device(): pl.pallas_call(kernel, out_shape=(jax.ShapeDtypeStruct((2, 1, 64, 256), B...]
where the time goes in v4:
time: 49.1 us; the launch traced here: 49 us
  Pallas kernels  48.4 us (99%)
  between operations  0.64 us (1%)
    pallas_call x1, Pallas kernels, on_device(): pl.pallas_call(kernel, out_shape=(jax.ShapeDtypeStruct((2, 1, 64, 256), B...  47.6 us

profile of v4, /device:TPU:1, one launch (start us, length us, event | category | flops | bytes accessed | tf_op | source)
XLA Modules:
  0.0 49.0 jit_solution(12104401956603146989)
XLA Ops:
  0.6 47.6 %shard_map.58 = (bf16[2,1,64,256]{3,2,1,0:T(8,128)(2,1)S(1)}, bf16[2,1,64,256]{3,2,1,0:T(8,128)(2,1)S(1)}, f32[8,9,128]{2,1,0:T(8,128)S(1)}, f32[8,18,128]{2,1,0:T(8,128)S(1)}) custom-call(bf16[2,1,64,256]{3,2,1,0:T(8,128)(2,1)} %act_hbm.1, bf16[27,256,256]{2,1,0:T(8,128)(2,1)} %w_hbm.1, bf16[2,1,64,256]{3,2,1,0:T(8,128)(2,1)} %grad_hbm.1), custom_call_target="tpu_custom_call" | custom-call | tf_op jit(solution)/shard_map/pallas_call | solution.py:393
  48.3 0.7 %shard_map.59 = (bf16[2,1,64,256]{3,2,1,0:T(8,128)(2,1)}, bf16[2,1,64,256]{3,2,1,0:T(8,128)(2,1)}, f32[27,4,256]{2,1,0:T(4,128)}) custom-call(bf16[2,1,64,256]{3,2,1,0:T(8,128)(2,1)S(1)} %get-tuple-element.7.out_v, bf16[2,1,64,256]{3,2,1,0:T(8,128)(2,1)S(1)} %get-tuple-element.8.gin_v, f32[8,9,128]{2,1,0:T(8,128)S(1)} %get-tuple-element.9.centre, ...), custom_call_target="tpu_custom_call" | custom-call | tf_op jit(solution)/shard_map/pallas_call | solution.py:436

commit v5 on v4

--- a/solution.py
+++ b/solution.py
@@ -38,6 +38,8 @@
         return (line * 2 + side, depth)
 
     def away(k, count):
+        if isinstance(k, int):
+            return count // 2 + (-((k + 1) // 2) if k % 2 else k // 2)
         return count // 2 + jnp.where(k % 2 == 0, k // 2, -((k + 1) // 2))
 
     own_grad = pltpu.make_async_copy(grad_hbm.at[:, 0], grad_halo.at[pl.ds(1, 2), 1], in_sem.at[0])
@@ -206,9 +208,11 @@
         return step
 
     act_here.start()
-    lax.fori_loop(0, 15, start(act_copy), 0)
-
-    lax.fori_loop(0, 7, start(grad_copy), 0)
+    for k in range(15):
+        act_copy(k).start()
+
+    for k in range(7):
+        grad_copy(k).start()
 
     def build_lhs(row, sides):
         here = act_all[row].astype(F32)
@@ -296,14 +300,16 @@
         for tap in range(3):
             centre[k, 3 * tap : 3 * tap + 3] = product[tap, pl.ds(k, 3, stride=32)]
     pltpu.make_async_copy(centre.at[m], centre_in.at[m], b_recv.at[0]).start()
-    lax.fori_loop(0, LINES - 1, start(centre_copy), 0)
+    for k in range(LINES - 1):
+        centre_copy(k).start()
 
     multiply(side_rows, 1 - c, False)
     for k in range(LINES):
         for tap in range(3):
             sides[k, 6 * tap : 6 * tap + 6] = product[tap, pl.ds(96 + k, 6, stride=32)]
     pltpu.make_async_copy(sides.at[m], sides_in.at[m], b_recv.at[1]).start()
-    lax.fori_loop(0, LINES - 1, start(sides_copy), 0)
+    for k in range(LINES - 1):
+        sides_copy(k).start()
 
     own_w.wait()
     for which in both:

time: 49.1 us -> 48.6 us (0.990)
  Pallas kernels: 48.4 us -> 47.9 us
where the time goes in v5:
time: 48.6 us; the launch traced here: 48.5 us
  Pallas kernels  47.9 us (99%)
  between operations  0.64 us (1%)
    pallas_call x1, Pallas kernels, on_device(): pl.pallas_call(kernel, out_shape=(jax.ShapeDtypeStruct((2, 1, 64, 256), B...  47.2 us

profile of v5, /device:TPU:1, one launch (start us, length us, event | category | flops | bytes accessed | tf_op | source)
XLA Modules:
  0.0 48.5 jit_solution(16230103745025440825)
XLA Ops:
  0.6 47.2 %shard_map.58 = (bf16[2,1,64,256]{3,2,1,0:T(8,128)(2,1)S(1)}, bf16[2,1,64,256]{3,2,1,0:T(8,128)(2,1)S(1)}, f32[8,9,128]{2,1,0:T(8,128)S(1)}, f32[8,18,128]{2,1,0:T(8,128)S(1)}) custom-call(bf16[2,1,64,256]{3,2,1,0:T(8,128)(2,1)} %act_hbm.1, bf16[27,256,256]{2,1,0:T(8,128)(2,1)} %w_hbm.1, bf16[2,1,64,256]{3,2,1,0:T(8,128)(2,1)} %grad_hbm.1), custom_call_target="tpu_custom_call" | custom-call | tf_op jit(solution)/shard_map/pallas_call | solution.py:399
  47.8 0.7 %shard_map.59 = (bf16[2,1,64,256]{3,2,1,0:T(8,128)(2,1)}, bf16[2,1,64,256]{3,2,1,0:T(8,128)(2,1)}, f32[27,4,256]{2,1,0:T(4,128)}) custom-call(bf16[2,1,64,256]{3,2,1,0:T(8,128)(2,1)S(1)} %get-tuple-element.7.out_v, bf16[2,1,64,256]{3,2,1,0:T(8,128)(2,1)S(1)} %get-tuple-element.8.gin_v, f32[8,9,128]{2,1,0:T(8,128)S(1)} %get-tuple-element.9.centre, ...), custom_call_target="tpu_custom_call" | custom-call | tf_op jit(solution)/shard_map/pallas_call | solution.py:442
